TPU v7x, 32 devices: a whole 2x2x4 slice. The times are simulated.
32 devices in a mesh: seq: 4 (over z), head: 8 (over y, x, core).
Axes of the slice: x: 2, y: 2, z: 4, core: 2. Of those that a mesh axis runs over, the one named last changes fastest.
Arguments:
- query_raw: bfloat16 [4096, 8192], P('seq', 'head'), may hold values from -12 to 12
- key_raw: bfloat16 [4096, 8192], P('seq', 'head'), may hold values from -6 to 6
- value_raw: bfloat16 [4096, 8192], P('seq', 'head'), may hold values from -6 to 6
- query_gain: float32 [8192], P('head'), may hold values from 0.1 to 1.9
- log_decay: float32 [64, 4096], P('head', 'seq'), may hold values from -1.5 to 0
- out_grad: bfloat16 [4096, 8192], P('seq', 'head'), may hold values from -0.75 to 0.75
Outputs:
- query_raw_grad: bfloat16 [4096, 8192], P(('seq', 'head'))
- key_raw_grad: bfloat16 [4096, 8192], P(('seq', 'head'))
- value_raw_grad: bfloat16 [4096, 8192], P(('seq', 'head'))
All inputs are finite; a program needn't handle non-finite values.
Results may differ from a plain program's by a relative error of at most 0.0021.
Values may be sent and summed in bfloat16 or wider, within the bound.
A program may use at most 128 MiB of HBM per device.

v0:
```python
import jax
import jax.numpy as jnp
from jax import lax
from jax.sharding import PartitionSpec as P

D = 8192
BLOCK = 128


epsilon = 1e-06


def from_behind(value, axis, steps):
    count = lax.axis_size(axis)
    initial, last = (max(0, -steps), min(count, count - steps))
    return lax.ppermute(value, axis, [(source, source + steps) for source in range(initial, last)])


def exact_prod(form, left, right):
    return jnp.einsum(form, left, right, precision=lax.Precision.HIGHEST)


def block_parts(queries, keys, gates):
    size = gates.shape[0]
    cumul = jnp.cumsum(gates)
    element_slot = lax.broadcasted_iota(jnp.int32, (size, size), 0)
    column = lax.broadcasted_iota(jnp.int32, (size, size), 1)
    causal = element_slot >= column
    strict = element_slot > column
    spread = jnp.where(causal, cumul[:, None] - cumul[None, :], 0.0)
    weights = jnp.where(causal, jnp.exp(spread), 0.0)
    lower = jnp.where(strict, 2.0 * weights * exact_prod("ik,jk->ij", keys, keys), 0.0)
    system = lower + jnp.eye(size, dtype=jnp.float32)
    mixing = 2.0 * weights * exact_prod("ik,jk->ij", queries, keys)
    start_decay = jnp.exp(cumul)
    end_decay = jnp.exp(cumul[-1] - cumul)
    return (system, mixing, start_decay, end_decay, start_decay[-1])


def solve_lower(system, target):
    return lax.linalg.triangular_solve(
        system, target, left_side=True, lower=True, unit_diagonal=True
    )


def block_forward(queries, keys, values, start_state, gates):
    system, mixing, start_decay, end_decay, total = block_parts(queries, keys, gates)
    target = values - start_decay[:, None] * exact_prod("ik,kv->iv", keys, start_state)
    fresh = solve_lower(system, target)
    outputs = start_decay[:, None] * exact_prod("ik,kv->iv", queries, start_state) + exact_prod(
        "ij,jv->iv", mixing, fresh
    )
    end_state = total * start_state + 2.0 * exact_prod(
        "ik,iv->kv", keys, end_decay[:, None] * fresh
    )
    return (outputs, end_state)


def block_maps(queries, keys, values, gates, grad_out):
    system, mixing, start_decay, end_decay, total = block_parts(queries, keys, gates)
    width = keys.shape[1]
    both = solve_lower(system, jnp.concatenate([values, start_decay[:, None] * keys], axis=1))
    initial_amount = both[:, : values.shape[1]]
    weight = both[:, values.shape[1] :]
    transition = total * jnp.eye(width, dtype=jnp.float32) - 2.0 * exact_prod(
        "ik,ij->kj", keys, end_decay[:, None] * weight
    )
    displacement = 2.0 * exact_prod("ik,iv->kv", keys, end_decay[:, None] * initial_amount)
    inner = exact_prod("ij,iv->jv", mixing, grad_out)
    adjoint = exact_prod("ik,iv->kv", start_decay[:, None] * queries, grad_out) - exact_prod(
        "jk,jv->kv", weight, inner
    )
    return (transition, displacement, adjoint)


def block_grads(queries, keys, values, start_state, gates, grad_out, end_grad):

    def forward(query_part, key_part, value_part):
        return block_forward(query_part, key_part, value_part, start_state, gates)

    _, pullback = jax.vjp(forward, queries, keys, values)
    return pullback((grad_out, end_grad))


def batched(function):
    return jax.vmap(jax.vmap(function))


def compose(earlier, later):
    return (
        exact_prod("hij,hjk->hik", later[0], earlier[0]),
        exact_prod("hij,hjk->hik", later[0], earlier[1]) + later[1],
    )


def per_device(query_raw, key_raw, value_raw, query_gain, log_decay, out_grad):
    rows, width = query_raw.shape
    heads = log_decay.shape[0]
    head_dim = width // heads
    blocks = rows // BLOCK
    raw_query = query_raw.astype(jnp.float32)
    squares = lax.psum(jnp.sum(raw_query * raw_query, axis=1), "head")
    inv_rms = lax.rsqrt(squares / D + epsilon)
    normed = raw_query * inv_rms[:, None]
    scale = head_dim ** (-0.5)
    queries = normed * query_gain * scale
    raw_key = key_raw.astype(jnp.float32).reshape(rows, heads, head_dim)
    key_scale = lax.rsqrt(jnp.sum(raw_key * raw_key, axis=2, keepdims=True) + epsilon)
    keys = raw_key * key_scale

    def to_blocks(array):
        return array.reshape(blocks, BLOCK, heads, head_dim).transpose(2, 0, 1, 3)

    query_blocks = to_blocks(queries)
    key_blocks = to_blocks(keys)
    value_blocks = to_blocks(value_raw.astype(jnp.float32))
    grad_blocks = to_blocks(out_grad.astype(jnp.float32))
    gate_blocks = log_decay.reshape(heads, blocks, BLOCK)
    transitions, displacements, adjoints = batched(block_maps)(
        query_blocks, key_blocks, value_blocks, gate_blocks, grad_blocks
    )
    trans_seq = jnp.moveaxis(transitions, 1, 0)
    offset_seq = jnp.moveaxis(displacements, 1, 0)
    adjoint_seq = jnp.moveaxis(adjoints, 1, 0)
    identity = jnp.broadcast_to(jnp.eye(head_dim, dtype=jnp.float32), (heads, head_dim, head_dim))
    zeros = jnp.zeros((heads, head_dim, head_dim), jnp.float32)

    def gather_step(carry, item):
        return (compose(carry, item), None)

    (device_map, device_offset), _ = lax.scan(
        gather_step, (identity, zeros), (trans_seq, offset_seq)
    )

    def collect_adjoint(carry, item):
        matrix, term = item
        return (exact_prod("hji,hjk->hik", matrix, carry) + term, None)

    device_adjoint, _ = lax.scan(collect_adjoint, zeros, (trans_seq, adjoint_seq), reverse=True)

    def forward_turn(step, received):
        sent = exact_prod("hij,hjk->hik", device_map, received) + device_offset
        return from_behind(sent, "seq", 1)

    def backward_turn(step, received):
        sent = exact_prod("hji,hjk->hik", device_map, received) + device_adjoint
        return from_behind(sent, "seq", -1)

    incoming = lax.fori_loop(0, lax.axis_size("seq") - 1, forward_turn, zeros)
    outgoing = lax.fori_loop(0, lax.axis_size("seq") - 1, backward_turn, zeros)

    def advance(state_matrix, item):
        matrix, shift = item
        return (exact_prod("hij,hjk->hik", matrix, state_matrix) + shift, state_matrix)

    def retreat(adjoint_state, item):
        matrix, term = item
        return (exact_prod("hji,hjk->hik", matrix, adjoint_state) + term, adjoint_state)

    _, starts = lax.scan(advance, incoming, (trans_seq, offset_seq))
    _, ends = lax.scan(retreat, outgoing, (trans_seq, adjoint_seq), reverse=True)
    query_grad, key_grad, value_grad = batched(block_grads)(
        query_blocks,
        key_blocks,
        value_blocks,
        jnp.moveaxis(starts, 0, 1),
        gate_blocks,
        grad_blocks,
        jnp.moveaxis(ends, 0, 1),
    )

    def from_blocks(array):
        return array.transpose(1, 2, 0, 3).reshape(rows, width)

    key_grad_rows = key_grad.transpose(1, 2, 0, 3).reshape(rows, heads, head_dim)
    key_raw_grad = key_scale * (
        key_grad_rows - keys * jnp.sum(keys * key_grad_rows, axis=2, keepdims=True)
    )
    key_raw_grad = key_raw_grad.reshape(rows, width).astype(jnp.bfloat16)
    value_raw_grad = from_blocks(value_grad).astype(jnp.bfloat16)
    scaled = from_blocks(query_grad) * query_gain * scale
    correction = lax.psum(jnp.sum(scaled * normed, axis=1), "head") / D
    query_raw_grad = (inv_rms[:, None] * (scaled - normed * correction[:, None])).astype(
        jnp.bfloat16
    )
    return (
        lax.all_to_all(query_raw_grad, "head", split_axis=0, concat_axis=1, tiled=True),
        lax.all_to_all(key_raw_grad, "head", split_axis=0, concat_axis=1, tiled=True),
        lax.all_to_all(value_raw_grad, "head", split_axis=0, concat_axis=1, tiled=True),
    )


def solution(mesh):
    in_specs = (
        P("seq", "head"),
        P("seq", "head"),
        P("seq", "head"),
        P("head"),
        P("head", "seq"),
        P("seq", "head"),
    )
    out_specs = (P(("seq", "head"), None), P(("seq", "head"), None), P(("seq", "head"), None))
    return jax.shard_map(
        per_device, mesh=mesh, in_specs=in_specs, out_specs=out_specs, check_vma=False
    )
```

profile of v0, /device:TPU:1, one launch (start us, length us, event | category | flops | bytes accessed | tf_op | source)
XLA Modules:
  0.0 1227.8 jit_solution(385944676142985091)
XLA Ops:
  30.4 12.2 add_bitcast_fusion.2
  42.6 630.2 %custom-call.8 = f32[8,8,1,128,128]{3,4,2,1,0:T(8,128)} custom-call(f32[8,8,1,128,128]{4,3,2,1,0:T(8,128)} %add_bitcast_fusion.2), custom_call_target="InvertDiagBlocksLowerTriangular" | custom-call | tf_op jit(solution)/shard_map/vmap(vmap())/triangular_solve | solution.py:41
  681.0 11.1 fusion.24
  692.1 11.2 multiply_bitcast_fusion.1
  719.0 29.4 %while.80 = (s32[]{:T(128)}, f32[8,128,128]{2,1,0:T(8,128)S(1)}, f32[8,128,128]{2,1,0:T(8,128)S(1)}, f32[8,8,128,128]{3,2,1,0:T(8,128)}, f32[8,8,128,128]{3,2,1,0:T(8,128)}, /*index=5*/s32[]{:T(128)}, s32[]{:T(128)}) while((s32[]{:T(128)}, f32[8,128,128]{2,1,0:T(8,128)S(1)}, f32[8,128,128]{2,1,0:T(8,128)S(1)}, ...), condition=%wide.region_5.6_spmd.clone, body=%wide.region_4.5_spmd.clone.sunk | while | flops 402915328 | bytes 5768791 | solution.py:131
  748.5 43.2 %while.76 = (s32[]{:T(128)}, f32[8,128,128]{2,1,0:T(8,128)S(1)}, f32[8,128,128]{2,1,0:T(8,128)S(1)}, f32[8,128,128]{2,1,0:T(8,128)S(1)}, s32[]{:T(128)}) while((s32[]{:T(128)}, f32[8,128,128]{2,1,0:T(8,128)S(1)}, f32[8,128,128]{2,1,0:T(8,128)S(1)}, f32[8,128,128]{2,1,0:T(8,128)S(1)}, s32[]{:T(128)}) %tuple.153), condition=%wide.region_7.8_spmd, body=%wide.region_6.7_spmd.sunk | while | flops 201457664 | bytes 4194405 | solution.py:149
  753.2 10.5 collective-permute-done
  794.2 22.0 %while.77 = (s32[]{:T(128)}, f32[8,128,128]{2,1,0:T(8,128)S(1)}, f32[8,8,128,128]{3,2,1,0:T(8,128)}, f32[8,8,128,128]{3,2,1,0:T(8,128)}, f32[8,8,128,128]{3,2,1,0:T(8,128)}, /*index=5*/s32[]{:T(128)}) while((s32[]{:T(128)}, f32[8,128,128]{2,1,0:T(8,128)S(1)}, f32[8,8,128,128]{3,2,1,0:T(8,128)}, f32[8,8,128,128]{3,2,1,0:T(8,128)}, ...), condition=%wide.region_9.10_spmd, body=%wide.region_8.9_spmd.sunk | while | flops 201457664 | bytes 4195909 | solution.py:160
  858.3 14.5 %psum.14 = f32[1024]{0:T(1024)S(1)} all-reduce(f32[1024]{0:T(1024)S(1)} %fusion.37), channel_id=1, replica_groups=mesh['seq'=4,'head'=8] {'head'}, use_global_device_ids=true, to_apply=%region_1.0 | all-reduce | flops 1024 | bytes 8192 | tf_op jit(solution)/shard_map/psum | solution.py:102
  876.9 11.8 psum.15
  896.7 11.1 fusion.47
  939.9 15.4 %while.81 = (s32[]{:T(128)}, f32[8,128,128]{2,1,0:T(8,128)S(1)}, f32[8,8,128,128]{2,3,1,0:T(8,128)}, f32[8,8,128,128]{3,2,1,0:T(8,128)}, s32[]{:T(128)}, /*index=5*/s32[]{:T(128)}, s32[]{:T(128)}) while((s32[]{:T(128)}, f32[8,128,128]{2,1,0:T(8,128)S(1)}, f32[8,8,128,128]{2,3,1,0:T(8,128)}, f32[8,8,128,128]{3,2,1,0:T(8,128)}, ...), condition=%wide.region_13.14_spmd.clone, body=%wide.region_12.13_spmd.clone.sunk | while | flops 201588736 | bytes 3147362 | solution.py:139
  955.3 44.7 %while.78 = (s32[]{:T(128)}, f32[8,128,128]{2,1,0:T(8,128)S(1)}, f32[8,128,128]{1,2,0:T(8,128)S(1)}, f32[8,128,128]{2,1,0:T(8,128)S(1)}, s32[]{:T(128)}) while((s32[]{:T(128)}, f32[8,128,128]{2,1,0:T(8,128)S(1)}, f32[8,128,128]{1,2,0:T(8,128)S(1)}, f32[8,128,128]{2,1,0:T(8,128)S(1)}, s32[]{:T(128)}) %tuple.172), condition=%wide.region_15.16_spmd, body=%wide.region_14.15_spmd.sunk | while | flops 201457664 | bytes 4194405 | solution.py:150
  957.3 14.4 %collective-permute-done.1 = f32[8,128,128]{2,1,0:T(8,128)S(1)} collective-permute-done((f32[8,128,128]{2,1,0:T(8,128)S(1)}, f32[8,128,128]{2,1,0:T(8,128)S(1)}, u32[]{:S(2)}, u32[]{:S(2)}) %collective-permute-start.1) | collective-permute-done | bytes 524320 | tf_op jit(solution)/shard_map/while/body/eval_jaxpr/ppermute | solution.py:16
  973.6 12.7 %collective-permute-done.1 = f32[8,128,128]{2,1,0:T(8,128)S(1)} collective-permute-done((f32[8,128,128]{2,1,0:T(8,128)S(1)}, f32[8,128,128]{2,1,0:T(8,128)S(1)}, u32[]{:S(2)}, u32[]{:S(2)}) %collective-permute-start.1) | collective-permute-done | bytes 524320 | tf_op jit(solution)/shard_map/while/body/eval_jaxpr/ppermute | solution.py:16
  988.3 11.8 collective-permute-done.1
  1002.5 22.1 %while.79 = (s32[]{:T(128)}, f32[8,128,128]{2,1,0:T(8,128)S(1)}, f32[8,8,128,128]{3,2,1,0:T(8,128)}, f32[8,8,128,128]{2,3,1,0:T(8,128)}, f32[8,8,128,128]{3,2,1,0:T(8,128)}, /*index=5*/s32[]{:T(128)}, s32[]{:T(128)}) while((s32[]{:T(128)}, f32[8,128,128]{2,1,0:T(8,128)S(1)}, f32[8,8,128,128]{3,2,1,0:T(8,128)}, ...), condition=%wide.region_17.18_spmd, body=%wide.region_16.17_spmd.sunk | while | flops 201457664 | bytes 4195421 | solution.py:161
  1033.3 10.6 fusion.78
  1052.2 10.3 fusion.158
  1067.8 11.3 fusion.73
  1105.4 16.2 %multiply_reduce_fusion = (f32[8,128,8]{1,0,2:T(8,128)S(1)}, f32[8,128,8,128]{3,1,0,2:T(8,128)}) fusion(f32[8,128,8]{1,0,2:T(8,128)S(1)} %copy.97, f32[8,128,8,128]{3,2,1,0:T(8,128)S(1)} %bitcast.250, f32[8,8,128,128]{3,2,1,0:T(8,128)} %fusion.57, f32[8,8,128,128]{3,2,1,0:T(8,128)} %copy-done.27, f32[8,8,128,128]{3,2,1,0:T(8,128)} %fusion.45, ...), kind=kOutput, calls=%fused_computation.95 | convolution fusion | flops 1618993152 | bytes 29425664 | tf_op jit(solution)/shard_map/vmap(vmap(transpose(jvp(ik,jk->ij))))/dot_general | solution.py:20
  1143.4 19.1 %all-to-all-done.1 = bf16[8,128,1024]{2,1,0:T(8,128)(2,1)S(1)} async-done(((bf16[8,128,1024]{2,1,0:T(8,128)(2,1)}), bf16[8,128,1024]{2,1,0:T(8,128)(2,1)S(1)}, u32[]{:S(2)}, u32[]{:S(2)}) %all-to-all-start.1) | async-done | bytes 2097184 | tf_op jit(solution)/shard_map/all_to_all | solution.py:188
  1162.5 33.1 %all_to_all.54 = bf16[8,128,1024]{1,2,0:T(8,128)(2,1)} all-to-all(bf16[8,128,1024]{1,2,0:T(8,128)(2,1)} %bitcast.269), channel_id=1, replica_groups=mesh['seq'=4,'head'=8] {'head'}, dimensions={0} | all-to-all | bytes 4194304 | tf_op jit(solution)/shard_map/all_to_all | solution.py:189
  1206.8 17.5 %all-to-all-done = bf16[8,128,1024]{2,1,0:T(8,128)(2,1)} async-done(((bf16[8,128,1024]{2,1,0:T(8,128)(2,1)}), bf16[8,128,1024]{2,1,0:T(8,128)(2,1)}, u32[]{:S(2)}, u32[]{:S(2)}) %all-to-all-start) | async-done | bytes 2097184 | tf_op jit(solution)/shard_map/all_to_all | solution.py:187
  (248 shorter events, 355.3 us)
Async XLA Ops:
  681.0 11.1 copy-start.1
  692.1 11.2 copy-start.10
  749.2 14.6 %collective-permute-start = (f32[8,128,128]{2,1,0:T(8,128)S(1)}, f32[8,128,128]{2,1,0:T(8,128)S(1)}, u32[]{:S(2)}, u32[]{:S(2)}) collective-permute-start(f32[8,128,128]{2,1,0:T(8,128)S(1)} %convolution_add_fusion.12), channel_id=1, source_target_pairs={{0,8},{8,16},{16,24},{1,9},{9,17},{17,25},{2,10},{10,18},{18,26},{... | collective-permute-start | bytes 1572872 | tf_op jit(solution)/shard_map/while/body/eval_jaxpr/ppermute | solution.py:16
  764.4 13.8 %collective-permute-start = (f32[8,128,128]{2,1,0:T(8,128)S(1)}, f32[8,128,128]{2,1,0:T(8,128)S(1)}, u32[]{:S(2)}, u32[]{:S(2)}) collective-permute-start(f32[8,128,128]{2,1,0:T(8,128)S(1)} %convolution_add_fusion.12), channel_id=1, source_target_pairs={{0,8},{8,16},{16,24},{1,9},{9,17},{17,25},{2,10},{10,18},{18,26},{... | collective-permute-start | bytes 1572872 | tf_op jit(solution)/shard_map/while/body/eval_jaxpr/ppermute | solution.py:16
  778.8 12.8 %collective-permute-start = (f32[8,128,128]{2,1,0:T(8,128)S(1)}, f32[8,128,128]{2,1,0:T(8,128)S(1)}, u32[]{:S(2)}, u32[]{:S(2)}) collective-permute-start(f32[8,128,128]{2,1,0:T(8,128)S(1)} %convolution_add_fusion.12), channel_id=1, source_target_pairs={{0,8},{8,16},{16,24},{1,9},{9,17},{17,25},{2,10},{10,18},{18,26},{... | collective-permute-start | bytes 1572872 | tf_op jit(solution)/shard_map/while/body/eval_jaxpr/ppermute | solution.py:16
  816.2 7.9 copy-start.12
  816.2 7.9 copy-start.20
  824.1 8.3 copy-start.32
  853.4 19.4 %copy-start.34 = (f32[1024]{0:T(1024)S(1)}, f32[1024]{0:T(1024)}, u32[]{:S(2)}) copy-start(f32[1024]{0:T(1024)} %param.23) | copy-start | bytes 12292
  895.0 12.9 %copy-start.5 = (f32[128,8,8,128]{3,2,1,0:T(8,128)}, f32[128,8,8,128]{3,2,1,0:T(8,128)S(1)}, u32[]{:S(2)}) copy-start(f32[128,8,8,128]{3,2,1,0:T(8,128)S(1)} %copy.174) | copy-start | bytes 12582916
  927.4 10.1 copy-start.28
  939.9 15.4 %copy-start.25 = (f32[8,128,128]{1,2,0:T(8,128)S(1)}, f32[8,128,128]{1,2,0:T(8,128)}, u32[]{:S(2)}) copy-start(f32[8,128,128]{1,2,0:T(8,128)} %copy.121) | copy-start | bytes 1572868
  956.0 15.7 %collective-permute-start.1 = (f32[8,128,128]{2,1,0:T(8,128)S(1)}, f32[8,128,128]{2,1,0:T(8,128)S(1)}, u32[]{:S(2)}, u32[]{:S(2)}) collective-permute-start(f32[8,128,128]{2,1,0:T(8,128)S(1)} %convolution_add_fusion.14), channel_id=1, source_target_pairs={{8,0},{16,8},{24,16},{9,1},{17,9},{25,17},{10,2},{18,10},{26,18},{... | collective-permute-start | bytes 1572872 | tf_op jit(solution)/shard_map/while/body/eval_jaxpr/ppermute | solution.py:16
  972.3 14.0 %collective-permute-start.1 = (f32[8,128,128]{2,1,0:T(8,128)S(1)}, f32[8,128,128]{2,1,0:T(8,128)S(1)}, u32[]{:S(2)}, u32[]{:S(2)}) collective-permute-start(f32[8,128,128]{2,1,0:T(8,128)S(1)} %convolution_add_fusion.14), channel_id=1, source_target_pairs={{8,0},{16,8},{24,16},{9,1},{17,9},{25,17},{10,2},{18,10},{26,18},{... | collective-permute-start | bytes 1572872 | tf_op jit(solution)/shard_map/while/body/eval_jaxpr/ppermute | solution.py:16
  987.0 13.1 %collective-permute-start.1 = (f32[8,128,128]{2,1,0:T(8,128)S(1)}, f32[8,128,128]{2,1,0:T(8,128)S(1)}, u32[]{:S(2)}, u32[]{:S(2)}) collective-permute-start(f32[8,128,128]{2,1,0:T(8,128)S(1)} %convolution_add_fusion.14), channel_id=1, source_target_pairs={{8,0},{16,8},{24,16},{9,1},{17,9},{25,17},{10,2},{18,10},{26,18},{... | collective-permute-start | bytes 1572872 | tf_op jit(solution)/shard_map/while/body/eval_jaxpr/ppermute | solution.py:16
  1024.6 8.7 copy-start.9
  1024.6 8.7 copy-start.18
  1033.3 10.6 copy-start.13
  1067.8 11.4 copy-start.6
  1081.4 9.9 copy-start.14
  1081.4 9.9 copy-start.31
  1091.3 8.0 copy-start.4
  1132.7 29.8 %all-to-all-start.1 = ((bf16[8,128,1024]{2,1,0:T(8,128)(2,1)}), bf16[8,128,1024]{2,1,0:T(8,128)(2,1)S(1)}, u32[]{:S(2)}, u32[]{:S(2)}) async-start(bf16[8,128,1024]{2,1,0:T(8,128)(2,1)} %bitcast.270), calls=%async_computation.1 | async-start | bytes 4194304 | tf_op jit(solution)/shard_map/all_to_all | solution.py:188
  1195.6 28.7 %all-to-all-start = ((bf16[8,128,1024]{2,1,0:T(8,128)(2,1)}), bf16[8,128,1024]{2,1,0:T(8,128)(2,1)}, u32[]{:S(2)}, u32[]{:S(2)}) async-start(bf16[8,128,1024]{2,1,0:T(8,128)(2,1)} %bitcast.20), calls=%async_computation | async-start | bytes 4194304 | tf_op jit(solution)/shard_map/all_to_all | solution.py:187
  (19 other events, 84.6 us)
where the time goes:
time: 1240 us; the launch traced here: 1230 us
  other arithmetic  667 us (54%)
  matrix products  279 us (22%)
  waiting for transfers between devices  104 us (8%)
  local copies, waits for them, and re-layouts  86.3 us (7%)
  blocking collectives  59.5 us (5%)
  starting transfers between devices  28.5 us (2%)
    another operation x4, other arithmetic, solve_lower(): lax.linalg.triangular_solve(system, target, left_side=True, lower=True, u...  630 us
    dot_general x63, matrix products, exact_prod(): return jnp.einsum(form, left, right, precision=lax.Precision.HIGHEST)  235 us
    ppermute x6, waiting for transfers between devices, from_behind(): lax.ppermute(value, axis, [(source, source + steps) for source in range(i...  67.6 us
    unnamed x80, local copies, waits for them, and re-layouts  38.7 us
    another operation x4, matrix products, solve_lower(): lax.linalg.triangular_solve(system, target, left_side=True, lower=True, u...  33.7 us
    all_to_all x1, blocking collectives, per_device(): lax.all_to_all(value_raw_grad, 'head', split_axis=0, concat_axis=1, tiled...  33.1 us
  transfers between devices with their start and end apart: 8, of which 8 were waited for; matrix products, arithmetic and copies ran while one was open for 1% of the time, Pallas kernels for 0%

commit v1 on v0

v1 whole, which is shorter than its diff:
```python
import math

import jax
import jax.numpy as jnp
from jax import lax
from jax.experimental import pallas as pl
from jax.experimental.pallas import tpu as pltpu
from jax.sharding import PartitionSpec as P

BLOCK = 128
GROUP = 4
VMEM = 48 * 1024 * 1024

epsilon = 1e-06


def parts(x):
    if isinstance(x, tuple):
        return x
    if x.dtype == jnp.bfloat16:
        return (x,)
    high = x.astype(jnp.bfloat16)
    return (high, (x - high.astype(jnp.float32)).astype(jnp.bfloat16))


def prod(a, b, ca=1, cb=0):
    a, b = parts(a), parts(b)
    pairs = [(x, y) for i, x in enumerate(a) for j, y in enumerate(b) if i + j < 2]
    left = pairs[0][0] if len(pairs) == 1 else jnp.concatenate([x for x, _ in pairs], axis=ca)
    right = pairs[0][1] if len(pairs) == 1 else jnp.concatenate([y for _, y in pairs], axis=cb)
    return lax.dot_general(
        left, right, (((ca,), (cb,)), ((), ())), preferred_element_type=jnp.float32
    )


def slots():
    row = lax.broadcasted_iota(jnp.int32, (BLOCK, BLOCK), 0)
    column = lax.broadcasted_iota(jnp.int32, (BLOCK, BLOCK), 1)
    return row, column


def each(function, *lists):
    return [function(*items) for items in zip(*lists)]


def lanes(ref, group):
    return [ref[:, h * BLOCK : (h + 1) * BLOCK] for h in range(group)]


def key_scales(keys):
    row, column = slots()

    def one(key):
        gram = prod(key, key, 1, 1)
        diag = jnp.where(row == column, gram, 0.0)
        return (
            gram,
            lax.rsqrt(jnp.sum(diag, axis=1, keepdims=True) + epsilon),
            lax.rsqrt(jnp.sum(diag, axis=0, keepdims=True) + epsilon),
        )

    return [one(key) for key in keys]


def decays(crow_ref, ccol_ref, group):
    row, column = slots()
    result = []
    for h in range(group):
        crow = crow_ref[h]
        ccol = ccol_ref[0, :, h : h + 1]
        last = crow[:, BLOCK - 1 :]
        weight = jnp.where(
            row >= column, 2.0 * jnp.exp(jnp.where(row >= column, ccol - crow, 0.0)), 0.0
        )
        result.append((weight, jnp.exp(ccol), jnp.exp(last - ccol), jnp.exp(last)))
    return result


def maps_kernel(k_ref, v_ref, crow_ref, ccol_ref, t_ref, w_ref, u_ref, a_ref, b_ref):
    group = crow_ref.shape[0]
    row, column = slots()
    eye = jnp.where(row == column, 1.0, 0.0)
    keys = lanes(k_ref, group)
    values = lanes(v_ref, group)
    scales = key_scales(keys)
    decay = decays(crow_ref, ccol_ref, group)

    def system(scale, dec):
        return jnp.where(row > column, dec[0] * scale[0] * scale[1] * scale[2], 0.0)

    lower = each(system, scales, decay)

    def pick(x, size):
        inside = (row // (2 * size)) == (column // (2 * size))
        across = (row // size) != (column // size)
        return jnp.where(inside & across, x, 0.0)

    inverse = [eye - pick(x, 1) for x in lower]
    size = 2
    while size < BLOCK:
        split = [parts(x) for x in inverse]
        inner = [prod(pick(x, size), s) for x, s in zip(lower, split)]
        inverse = [t - prod(s, y) for t, s, y in zip(inverse, split, inner)]
        size *= 2
    for h in range(group):
        t_ref[h, 0] = inverse[h]
    crows = [crow_ref[h] for h in range(group)]
    weights = [
        prod(t * (jnp.exp(c) * s[2]), k) for t, c, s, k in zip(inverse, crows, scales, keys)
    ]
    initial = each(prod, inverse, values)
    ends = [d[2] * s[1] for d, s in zip(decay, scales)]
    both = [
        prod(k, 2.0 * e * jnp.concatenate([w, u], axis=1), 0, 0)
        for k, e, w, u in zip(keys, ends, weights, initial)
    ]
    for h in range(group):
        w_ref[h, 0] = weights[h]
        u_ref[h, 0] = initial[h]
        a_ref[h, 0] = decay[h][3] * eye - both[h][:, :BLOCK]
        b_ref[h, 0] = both[h][:, BLOCK:]


def chain_kernel(
    q_ref, k_ref, g_ref, crow_ref, ccol_ref, inv_ref, gain_ref, gcol_ref, w_ref, a_ref, b_ref,
    inner_ref, c_ref, pre_ref, map_ref, adj_ref,
):
    group = crow_ref.shape[0]
    row, column = slots()

    @pl.when(pl.program_id(1) == 0)
    def _():
        eye = jnp.where(row == column, 1.0, 0.0)
        for h in range(group):
            map_ref[h, :, :BLOCK] = eye
            map_ref[h, :, BLOCK:] = jnp.zeros((BLOCK, BLOCK), jnp.float32)
            adj_ref[h] = jnp.zeros((BLOCK, BLOCK), jnp.float32)

    queries = lanes(q_ref, group)
    keys = lanes(k_ref, group)
    grads = lanes(g_ref, group)
    gains = lanes(gain_ref, group)
    inv = inv_ref[...]
    scales = key_scales(keys)
    decay = decays(crow_ref, ccol_ref, group)
    mixing = [
        prod(q, k.astype(jnp.float32) * gs, 1, 1) * (d[0] * inv * s[2])
        for q, k, gs, d, s in zip(queries, keys, gains, decay, scales)
    ]
    inner = [prod(m, g, 0, 0) for m, g in zip(mixing, grads)]
    direct = [
        gcol_ref[h] * prod(queries[h], (decay[h][1] * inv) * grads[h].astype(jnp.float32), 0, 0)
        for h in range(group)
    ]
    adjoint = [direct[h] - prod(w_ref[h, 0], inner[h], 0, 0) for h in range(group)]
    for h in range(group):
        before = map_ref[h]
        pre_ref[h, 0] = before
        inner_ref[h, 0] = inner[h]
        c_ref[h, 0] = adjoint[h]
        adj_ref[h] += prod(before[:, :BLOCK], adjoint[h], 0, 0)
        after = prod(a_ref[h, 0], before)
        map_ref[h, :, :BLOCK] = after[:, :BLOCK]
        map_ref[h, :, BLOCK:] = after[:, BLOCK:] + b_ref[h, 0]


def grads_kernel(
    q_ref, k_ref, g_ref, crow_ref, ccol_ref, inv_ref, gain_ref,
    t_ref, w_ref, u_ref, a_ref, c_ref, inner_ref, pre_ref, in_ref, out_ref,
    dq_ref, dk_ref, dv_ref, corr_ref, carry_ref,
):
    group = crow_ref.shape[0]
    heads = range(group)
    row, column = slots()

    @pl.when(pl.program_id(1) == 0)
    def _():
        carry_ref[...] = out_ref[...]

    queries = lanes(q_ref, group)
    keys = lanes(k_ref, group)
    grads = lanes(g_ref, group)
    gains = lanes(gain_ref, group)
    inv = inv_ref[...]
    scales = key_scales(keys)
    decay = decays(crow_ref, ccol_ref, group)
    start = [
        parts(prod(pre_ref[h, 0, :, :BLOCK], in_ref[h]) + pre_ref[h, 0, :, BLOCK:]) for h in heads
    ]
    end = [parts(carry_ref[h]) for h in heads]
    fresh = [parts(u_ref[h, 0] - prod(w_ref[h, 0], start[h])) for h in heads]
    dfresh = [
        inner_ref[h, 0] + (2.0 * decay[h][2] * scales[h][1]) * prod(keys[h], end[h]) for h in heads
    ]
    for h in heads:
        carry_ref[h] = prod(a_ref[h, 0], end[h], 0, 0) + c_ref[h, 0]
    target = [prod(t_ref[h, 0], dfresh[h], 0, 0) for h in heads]
    tparts = [parts(x) for x in target]
    spread = [decay[h][0] * prod(grads[h], fresh[h], 1, 1) for h in heads]
    pairs = [
        jnp.where(row > column, decay[h][0] * prod(tparts[h], fresh[h], 1, 1), 0.0) for h in heads
    ]
    dquery = [
        decay[h][1] * prod(grads[h], start[h], 1, 1) + prod(spread[h] * scales[h][2], keys[h])
        for h in heads
    ]
    dkey = [
        2.0 * decay[h][2] * prod(fresh[h], end[h], 1, 1)
        - decay[h][1] * prod(tparts[h], start[h], 1, 1)
        for h in heads
    ]
    dkey = [
        dkey[h] - prod((pairs[h] + pairs[h].T) * scales[h][2], keys[h]) for h in heads
    ]
    dkey = [
        dkey[h] + gains[h] * prod(spread[h] * inv, queries[h], 0, 0) for h in heads
    ]
    total = jnp.zeros((BLOCK, 1), jnp.float32)
    for h in heads:
        span = slice(h * BLOCK, (h + 1) * BLOCK)
        scaled = dquery[h] * gains[h]
        dq_ref[:, span] = scaled
        total += jnp.sum(scaled * (queries[h].astype(jnp.float32) * inv), axis=1, keepdims=True)
        dv_ref[:, span] = target[h].astype(jnp.bfloat16)
        scale = scales[h][1]
        unit = keys[h].astype(jnp.float32) * scale
        along = jnp.sum(unit * dkey[h], axis=1, keepdims=True)
        dk_ref[:, span] = (scale * (dkey[h] - unit * along)).astype(jnp.bfloat16)
    corr_ref[0] = total


def shift(value, axis, steps):
    count = lax.axis_size(axis)
    first, last = (max(0, -steps), min(count, count - steps))
    return lax.ppermute(value, axis, [(i, i + steps) for i in range(first, last)])


def apply_map(form, matrix, state):
    return jnp.einsum(form, matrix, state, precision=lax.Precision.HIGHEST)


def per_device(query_raw, key_raw, value_raw, query_gain, log_decay, out_grad):
    rows, width = query_raw.shape
    heads = log_decay.shape[0]
    size = width // heads
    blocks = rows // BLOCK
    group = math.gcd(heads, GROUP)
    groups = heads // group
    full = width * lax.axis_size("head")
    f32 = jnp.float32

    raw_query = query_raw.astype(f32)
    squares = lax.psum(jnp.sum(raw_query * raw_query, axis=1), "head")
    inv = lax.rsqrt(squares / full + epsilon)[:, None]
    gain = query_gain * size ** (-0.5)
    gain_row = gain[None, :]
    gain_col = gain.reshape(heads, size, 1)
    cumul = jnp.cumsum(log_decay.reshape(heads, blocks, BLOCK), axis=2).reshape(heads, rows)
    crow = cumul[:, None, :]
    ccol = cumul.reshape(groups, group, rows).transpose(0, 2, 1)

    def specs(order):
        return dict(
            raw=pl.BlockSpec((BLOCK, group * size), lambda g, b: (order(b), g)),
            crow=pl.BlockSpec((group, 1, BLOCK), lambda g, b: (g, 0, order(b))),
            ccol=pl.BlockSpec((1, BLOCK, group), lambda g, b: (g, order(b), 0)),
            inv=pl.BlockSpec((BLOCK, 1), lambda g, b: (order(b), 0)),
            gain=pl.BlockSpec((1, group * size), lambda g, b: (0, g)),
            gcol=pl.BlockSpec((group, size, 1), lambda g, b: (g, 0, 0)),
            mat=pl.BlockSpec((group, 1, size, size), lambda g, b: (g, order(b), 0, 0)),
            pre=pl.BlockSpec((group, 1, size, 2 * size), lambda g, b: (g, order(b), 0, 0)),
            head=pl.BlockSpec((group, size, size), lambda g, b: (g, 0, 0)),
            map=pl.BlockSpec((group, size, 2 * size), lambda g, b: (g, 0, 0)),
            corr=pl.BlockSpec((1, BLOCK, 1), lambda g, b: (g, order(b), 0)),
        )

    grid = (groups, blocks)
    mat = jax.ShapeDtypeStruct((heads, blocks, size, size), f32)
    pre = jax.ShapeDtypeStruct((heads, blocks, size, 2 * size), f32)
    params = pltpu.CompilerParams(
        dimension_semantics=("arbitrary", "arbitrary"), vmem_limit_bytes=VMEM
    )

    def cost(passes):
        flops = 2 * passes * BLOCK**3 * heads * blocks
        return pl.CostEstimate(flops=flops, bytes_accessed=24 * 2**20, transcendentals=0)

    s = specs(lambda b: b)
    inverse, weight, initial, trans, offset = pl.pallas_call(
        maps_kernel,
        grid=grid,
        in_specs=[s["raw"], s["raw"], s["crow"], s["ccol"]],
        out_specs=[s["mat"]] * 5,
        out_shape=[mat] * 5,
        compiler_params=params,
        cost_estimate=cost(160),
        name="block_maps",
    )(key_raw, value_raw, crow, ccol)
    inner, adjoint, prefix, device_map, device_adjoint = pl.pallas_call(
        chain_kernel,
        grid=grid,
        in_specs=[s["raw"]] * 3
        + [s["crow"], s["ccol"], s["inv"], s["gain"], s["gcol"]]
        + [s["mat"]] * 3,
        out_specs=[s["mat"], s["mat"], s["pre"], s["map"], s["head"]],
        out_shape=[
            mat,
            mat,
            pre,
            jax.ShapeDtypeStruct((heads, size, 2 * size), f32),
            jax.ShapeDtypeStruct((heads, size, size), f32),
        ],
        compiler_params=params,
        cost_estimate=cost(80),
        name="device_maps",
    )(
        query_raw, key_raw, out_grad, crow, ccol, inv, gain_row, gain_col, weight, trans, offset
    )

    through, shifted = device_map[:, :, :size], device_map[:, :, size:]
    incoming = jnp.zeros((heads, size, size), f32)
    outgoing = jnp.zeros((heads, size, size), f32)
    for step in range(lax.axis_size("seq") - 1):
        ahead, back = shifted, device_adjoint
        if step:
            ahead = apply_map("hij,hjk->hik", through, incoming) + ahead
            back = apply_map("hji,hjk->hik", through, outgoing) + back
        incoming = shift(ahead, "seq", 1)
        outgoing = shift(back, "seq", -1)

    s = specs(lambda b: blocks - 1 - b)
    scaled, key_grad, value_grad, correction = pl.pallas_call(
        grads_kernel,
        grid=grid,
        in_specs=[s["raw"]] * 3
        + [s["crow"], s["ccol"], s["inv"], s["gain"]]
        + [s["mat"]] * 6
        + [s["pre"], s["head"], s["head"]],
        out_specs=[s["raw"], s["raw"], s["raw"], s["corr"]],
        out_shape=[
            jax.ShapeDtypeStruct((rows, width), f32),
            jax.ShapeDtypeStruct((rows, width), jnp.bfloat16),
            jax.ShapeDtypeStruct((rows, width), jnp.bfloat16),
            jax.ShapeDtypeStruct((groups, rows, 1), f32),
        ],
        scratch_shapes=[pltpu.VMEM((group, size, size), f32)],
        compiler_params=params,
        cost_estimate=cost(160),
        name="block_grads",
    )(
        query_raw, key_raw, out_grad, crow, ccol, inv, gain_row,
        inverse, weight, initial, trans, adjoint, inner, prefix, incoming, outgoing,
    )

    correction = lax.psum(jnp.sum(correction, axis=0), "head") / full
    query_grad = (inv * (scaled - raw_query * inv * correction)).astype(jnp.bfloat16)

    def to_owner(array):
        return lax.all_to_all(array, "head", split_axis=0, concat_axis=1, tiled=True)

    return to_owner(query_grad), to_owner(key_grad), to_owner(value_grad)


def solution(mesh):
    in_specs = (
        P("seq", "head"),
        P("seq", "head"),
        P("seq", "head"),
        P("head"),
        P("head", "seq"),
        P("seq", "head"),
    )
    out_specs = (P(("seq", "head"), None), P(("seq", "head"), None), P(("seq", "head"), None))
    return jax.shard_map(
        per_device, mesh=mesh, in_specs=in_specs, out_specs=out_specs, check_vma=False
    )
```

time: 1240 us -> 308 us (0.25)
  other arithmetic: 667 us -> 9.47 us
  matrix products: 279 us -> 3.4 us
  Pallas kernels: 0 us -> 122 us
  local copies, waits for them, and re-layouts: 86.3 us -> 13.5 us
  waiting for transfers between devices: 104 us -> 40.5 us
  blocking collectives: 59.5 us -> 94 us
    another operation x5 -> x1, other arithmetic: 633 us -> 2.26 us  [per_device(): jnp.cumsum(log_decay.reshape(heads, blocks, BLOCK), axis=2)]
    dot_general x64 -> x4, matrix products: 245 us -> 3.4 us  [apply_map(): return jnp.einsum(form, matrix, state, precision=lax.Precision.HIGHEST)]
    pallas_call x0 -> x3, Pallas kernels: none -> 122 us  [the longest x1 52.3 us: per_device(): pl.pallas_call(maps_kernel, grid=grid, in_specs=[s['raw'], s['raw'], s['c...]
    ppermute x6, waiting for transfers between devices: 67.6 us -> 22.2 us  [shift(): lax.ppermute(value, axis, [(i, i + steps) for i in range(first, last)])]
    another operation x4 -> x0, matrix products: 33.7 us -> none  [solve_lower(): lax.linalg.triangular_solve(system, target, left_side=True, lower=True, u...]
    unnamed x80 -> x20, local copies, waits for them, and re-layouts: 38.7 us -> 5.49 us
    all_to_all x1 -> x2, blocking collectives: 33.1 us -> 59.1 us  [to_owner(): lax.all_to_all(array, 'head', split_axis=0, concat_axis=1, tiled=True)]
    all_to_all x2 -> x1, waiting for transfers between devices: 36.6 us -> 18.3 us  [to_owner(): lax.all_to_all(array, 'head', split_axis=0, concat_axis=1, tiled=True)]
  transfers between devices with their start and end apart: 8 -> 7, of which waited for: 8 -> 6; matrix products, arithmetic and copies ran while one was open for 1% -> 3% of each run, Pallas kernels for 0% -> 0%
where the time goes in v1:
time: 308 us; the launch traced here: 304 us
  Pallas kernels  122 us (40%)
  blocking collectives  94 us (31%)
  waiting for transfers between devices  40.5 us (13%)
  starting transfers between devices  20.4 us (7%)
  local copies, waits for them, and re-layouts  13.5 us (4%)
  other arithmetic  9.47 us (3%)
  matrix products  3.4 us (1%)
    all_to_all x2, blocking collectives, to_owner(): lax.all_to_all(array, 'head', split_axis=0, concat_axis=1, tiled=True)  59.1 us
    pallas_call x1, Pallas kernels, per_device(): pl.pallas_call(maps_kernel, grid=grid, in_specs=[s['raw'], s['raw'], s['c...  52.3 us
    pallas_call x1, Pallas kernels, per_device(): pl.pallas_call(grads_kernel, grid=grid, in_specs=[s['raw']] * 3 + [s['cro...  36.5 us
    pallas_call x1, Pallas kernels, per_device(): pl.pallas_call(chain_kernel, grid=grid, in_specs=[s['raw']] * 3 + [s['cro...  32.8 us
    psum x1, blocking collectives, per_device(): correction = lax.psum(jnp.sum(correction, axis=0), 'head') / full  22.3 us
    ppermute x6, waiting for transfers between devices, shift(): lax.ppermute(value, axis, [(i, i + steps) for i in range(first, last)])  22.2 us
    all_to_all x1, waiting for transfers between devices, to_owner(): lax.all_to_all(array, 'head', split_axis=0, concat_axis=1, tiled=True)  18.3 us
    ppermute x6, starting transfers between devices, shift(): lax.ppermute(value, axis, [(i, i + steps) for i in range(first, last)])  15.6 us
  transfers between devices with their start and end apart: 7, of which 6 were waited for; matrix products, arithmetic and copies ran while one was open for 3% of the time, Pallas kernels for 0%

profile of v1, /device:TPU:1, one launch (start us, length us, event | category | flops | bytes accessed | tf_op | source)
XLA Modules:
  0.0 303.6 jit_solution(3780189610065984213)
XLA Ops:
  0.6 2.1 fusion
  2.7 12.6 %psum.14 = f32[1024]{0:T(1024)S(1)} all-reduce(f32[1024]{0:T(1024)S(1)} %fusion), channel_id=1, replica_groups=mesh['seq'=4,'head'=8] {'head'}, use_global_device_ids=true, to_apply=%region_1.0 | all-reduce | flops 1024 | bytes 8192 | tf_op jit(solution)/shard_map/psum | solution.py:253
  16.8 2.3 reduce_window_sum.11
  19.9 1.6 copy-done.7
  21.5 1.6 copy-done.8
  23.1 52.3 %block_maps.1 = (f32[8,8,128,128]{3,2,1,0:T(8,128)}, f32[8,8,128,128]{3,2,1,0:T(8,128)}, f32[8,8,128,128]{3,2,1,0:T(8,128)}, f32[8,8,128,128]{3,2,1,0:T(8,128)}, f32[8,8,128,128]{3,2,1,0:T(8,128)}) custom-call(bf16[1024,1024]{1,0:T(8,128)(2,1)S(1)} %copy-done.8, bf16[1024,1024]{1,0:T(8,128)(2,1)S(1)} %copy-done.7, f32[8,1,1024]{2,1,0:T(1,128)S(1)} %bitcast.29, ...), custom_call_target="tpu_custom_call" | custom-call | flops 42949672960 | bytes 25165824 | tf_op jit(solution)/shard_map/block_maps/pallas_call | solution.py:289
  75.3 32.8 %device_maps.1 = (f32[8,8,128,128]{3,2,1,0:T(8,128)}, f32[8,8,128,128]{3,2,1,0:T(8,128)}, f32[8,8,128,256]{3,2,1,0:T(8,128)}, f32[8,128,256]{2,1,0:T(8,128)S(1)}, f32[8,128,128]{2,1,0:T(8,128)S(1)}) custom-call(bf16[1024,1024]{1,0:T(8,128)(2,1)S(1)} %copy-done, bf16[1024,1024]{1,0:T(8,128)(2,1)} %k_ref.5, bf16[1024,1024]{1,0:T(8,128)(2,1)} %g_ref.3, ...), custom_call_target="tpu_custom_call" | custom-call | flops 21474836480 | bytes 25165824 | tf_op jit(solution)/shard_map/device_maps/pallas_call | solution.py:299
  108.2 3.4 %collective-permute-start = (f32[8,128,128]{2,1,0:T(8,128)S(1)}, f32[8,128,128]{2,1,0:T(8,128)S(1)}, u32[]{:S(2)}, u32[]{:S(2)}) collective-permute-start(f32[8,128,128]{2,1,0:T(8,128)S(1)} %slice.7), channel_id=1, source_target_pairs={{0,8},{8,16},{16,24},{1,9},{9,17},{17,25},{2,10},{10,18},{18,26},{... | collective-permute-start | bytes 1572872 | tf_op jit(solution)/shard_map/ppermute | solution.py:235
  112.9 7.3 %collective-permute-done = f32[8,128,128]{2,1,0:T(8,128)S(1)} collective-permute-done((f32[8,128,128]{2,1,0:T(8,128)S(1)}, f32[8,128,128]{2,1,0:T(8,128)S(1)}, u32[]{:S(2)}, u32[]{:S(2)}) %collective-permute-start) | collective-permute-done | bytes 524320 | tf_op jit(solution)/shard_map/ppermute | solution.py:235
  120.9 4.1 %collective-permute-start.1 = (f32[8,128,128]{2,1,0:T(8,128)S(1)}, f32[8,128,128]{2,1,0:T(8,128)S(1)}, u32[]{:S(2)}, u32[]{:S(2)}) collective-permute-start(f32[8,128,128]{2,1,0:T(8,128)S(1)} %convolution_add_fusion.3), channel_id=1, source_target_pairs={{0,8},{8,16},{16,24},{1,9},{9,17},{17,25},{2,10},{10,18},{18,26},{... | collective-permute-start | bytes 1572872 | tf_op jit(solution)/shard_map/ppermute | solution.py:235
  127.4 5.4 %collective-permute-done.1 = f32[8,128,128]{2,1,0:T(8,128)S(1)} collective-permute-done((f32[8,128,128]{2,1,0:T(8,128)S(1)}, f32[8,128,128]{2,1,0:T(8,128)S(1)}, u32[]{:S(2)}, u32[]{:S(2)}) %collective-permute-start.1) | collective-permute-done | bytes 524320 | tf_op jit(solution)/shard_map/ppermute | solution.py:235
  133.5 4.1 %collective-permute-start.2 = (f32[8,128,128]{2,1,0:T(8,128)S(1)}, f32[8,128,128]{2,1,0:T(8,128)S(1)}, u32[]{:S(2)}, u32[]{:S(2)}) collective-permute-start(f32[8,128,128]{2,1,0:T(8,128)S(1)} %convolution_add_fusion.2), channel_id=1, source_target_pairs={{0,8},{8,16},{16,24},{1,9},{9,17},{17,25},{2,10},{10,18},{18,26},{... | collective-permute-start | bytes 1572872 | tf_op jit(solution)/shard_map/ppermute | solution.py:235
  140.1 4.3 %collective-permute-done.2.in_ref = f32[8,128,128]{2,1,0:T(8,128)S(1)} collective-permute-done((f32[8,128,128]{2,1,0:T(8,128)S(1)}, f32[8,128,128]{2,1,0:T(8,128)S(1)}, u32[]{:S(2)}, u32[]{:S(2)}) %collective-permute-start.2) | collective-permute-done | bytes 524320 | tf_op jit(solution)/shard_map/ppermute | solution.py:235
  144.4 5.0 %collective-permute-done.5.out_ref = f32[8,128,128]{2,1,0:T(8,128)S(1)} collective-permute-done((f32[8,128,128]{2,1,0:T(8,128)S(1)}, f32[8,128,128]{2,1,0:T(8,128)S(1)}, u32[]{:S(2)}, u32[]{:S(2)}) %collective-permute-start.5) | collective-permute-done | bytes 524320 | tf_op jit(solution)/shard_map/ppermute | solution.py:235
  149.4 36.5 %block_grads.1 = (f32[1024,1024]{1,0:T(8,128)}, bf16[1024,1024]{1,0:T(8,128)(2,1)S(1)}, bf16[1024,1024]{1,0:T(8,128)(2,1)}, f32[2,1024,1]{2,1,0:T(8,128)S(1)}) custom-call(bf16[1024,1024]{1,0:T(8,128)(2,1)} %q_ref.3, bf16[1024,1024]{1,0:T(8,128)(2,1)} %k_ref.5, bf16[1024,1024]{1,0:T(8,128)(2,1)} %g_ref.3, f32[8,1,1024]{2,1,0:T(1,128)S(1)} %bitcast.31, ...), custom_call_target="tpu_custom_call" | custom-call | flops 42949672960 | bytes 25165824 | tf_op jit(solution)/shard_map/block_grads/pallas_call | solution.py:332
  189.6 22.3 %psum.15 = f32[1024,1]{0,1:T(1,128)S(1)} all-reduce(f32[1024,1]{0,1:T(1,128)S(1)} %bitcast.45), channel_id=1, replica_groups=mesh['seq'=4,'head'=8] {'head'}, use_global_device_ids=true, to_apply=%region_4.5 | all-reduce | flops 1024 | bytes 8192 | tf_op jit(solution)/shard_map/psum | solution.py:355
  211.9 3.0 fusion.4
  214.9 29.4 %all_to_all.57 = bf16[8,128,1024]{2,1,0:T(8,128)(2,1)} all-to-all(bf16[8,128,1024]{2,1,0:T(8,128)(2,1)S(1)} %bitcast.34), channel_id=1, replica_groups=mesh['seq'=4,'head'=8] {'head'}, dimensions={0} | all-to-all | bytes 4194304 | tf_op jit(solution)/shard_map/all_to_all | solution.py:359
  244.3 29.7 %all_to_all.58 = bf16[8,128,1024]{2,1,0:T(8,128)(2,1)} all-to-all(bf16[8,128,1024]{2,1,0:T(8,128)(2,1)S(1)} %bitcast.25), channel_id=1, replica_groups=mesh['seq'=4,'head'=8] {'head'}, dimensions={0} | all-to-all | bytes 4194304 | tf_op jit(solution)/shard_map/all_to_all | solution.py:359
  274.1 4.8 %all-to-all-start.2 = ((bf16[8,128,1024]{2,1,0:T(8,128)(2,1)}), bf16[8,128,1024]{2,1,0:T(8,128)(2,1)S(1)}, u32[]{:S(2)}, u32[]{:S(2)}) async-start(bf16[8,128,1024]{2,1,0:T(8,128)(2,1)} %bitcast.38), calls=%async_computation.2 | async-start | bytes 4194304 | tf_op jit(solution)/shard_map/all_to_all | solution.py:359
  278.9 3.3 %copy.24 = bf16[8,16,8,1024]{3,2,0,1:T(8,128)(2,1)} copy(bf16[8,16,8,1024]{3,2,1,0:T(8,128)(2,1)} %bitcast.36) | data formatting | bytes 4194304 | tf_op jit(solution)/shard_map/all_to_all | solution.py:359
  282.2 1.5 copy.25
  283.7 18.3 %all-to-all-done.2 = bf16[8,128,1024]{2,1,0:T(8,128)(2,1)S(1)} async-done(((bf16[8,128,1024]{2,1,0:T(8,128)(2,1)}), bf16[8,128,1024]{2,1,0:T(8,128)(2,1)S(1)}, u32[]{:S(2)}, u32[]{:S(2)}) %all-to-all-start.2) | async-done | bytes 2097184 | tf_op jit(solution)/shard_map/all_to_all | solution.py:359
  302.1 1.6 copy.26
  (37 shorter events, 13.5 us)
Async XLA Ops:
  19.5 55.8 %copy-start.5 = (f32[1024,1]{1,0:T(8,128)}, f32[1024,1]{1,0:T(8,128)S(1)}, u32[]{:S(2)}) copy-start(f32[1024,1]{1,0:T(8,128)S(1)} %copy.19.inv_ref) | copy-start | bytes 12292
  19.9 1.6 copy-start.7
  21.5 1.6 copy-start.8
  23.1 52.3 %copy-start = (bf16[1024,1024]{1,0:T(8,128)(2,1)S(1)}, bf16[1024,1024]{1,0:T(8,128)(2,1)}, u32[]{:S(2)}) copy-start(bf16[1024,1024]{1,0:T(8,128)(2,1)} %q_ref.3) | copy-start | bytes 6291460
  108.1 41.3 %copy-start.6 = (f32[1024,1]{1,0:T(8,128)S(1)}, f32[1024,1]{1,0:T(8,128)}, u32[]{:S(2)}) copy-start(f32[1024,1]{1,0:T(8,128)} %copy-done.5) | copy-start | bytes 12292
  108.2 12.1 %collective-permute-start = (f32[8,128,128]{2,1,0:T(8,128)S(1)}, f32[8,128,128]{2,1,0:T(8,128)S(1)}, u32[]{:S(2)}, u32[]{:S(2)}) collective-permute-start(f32[8,128,128]{2,1,0:T(8,128)S(1)} %slice.7), channel_id=1, source_target_pairs={{0,8},{8,16},{16,24},{1,9},{9,17},{17,25},{2,10},{10,18},{18,26},{... | collective-permute-start | bytes 1572872 | tf_op jit(solution)/shard_map/ppermute | solution.py:235
  111.6 13.5 %collective-permute-start.3 = (f32[8,128,128]{2,1,0:T(8,128)S(1)}, f32[8,128,128]{2,1,0:T(8,128)S(1)}, u32[]{:S(2)}, u32[]{:S(2)}) collective-permute-start(f32[8,128,128]{2,1,0:T(8,128)S(1)} %get-tuple-element.26), channel_id=1, source_target_pairs={{8,0},{16,8},{24,16},{9,1},{17,9},{25,17},{10,2},{18,10},{26,18},{... | collective-permute-start | bytes 1572872 | tf_op jit(solution)/shard_map/ppermute | solution.py:235
  120.9 11.9 %collective-permute-start.1 = (f32[8,128,128]{2,1,0:T(8,128)S(1)}, f32[8,128,128]{2,1,0:T(8,128)S(1)}, u32[]{:S(2)}, u32[]{:S(2)}) collective-permute-start(f32[8,128,128]{2,1,0:T(8,128)S(1)} %convolution_add_fusion.3), channel_id=1, source_target_pairs={{0,8},{8,16},{16,24},{1,9},{9,17},{17,25},{2,10},{10,18},{18,26},{... | collective-permute-start | bytes 1572872 | tf_op jit(solution)/shard_map/ppermute | solution.py:235
  126.1 11.6 %collective-permute-start.4 = (f32[8,128,128]{2,1,0:T(8,128)S(1)}, f32[8,128,128]{2,1,0:T(8,128)S(1)}, u32[]{:S(2)}, u32[]{:S(2)}) collective-permute-start(f32[8,128,128]{2,1,0:T(8,128)S(1)} %convolution_add_fusion.1), channel_id=1, source_target_pairs={{8,0},{16,8},{24,16},{9,1},{17,9},{25,17},{10,2},{18,10},{26,18},{... | collective-permute-start | bytes 1572872 | tf_op jit(solution)/shard_map/ppermute | solution.py:235
  133.5 10.9 %collective-permute-start.2 = (f32[8,128,128]{2,1,0:T(8,128)S(1)}, f32[8,128,128]{2,1,0:T(8,128)S(1)}, u32[]{:S(2)}, u32[]{:S(2)}) collective-permute-start(f32[8,128,128]{2,1,0:T(8,128)S(1)} %convolution_add_fusion.2), channel_id=1, source_target_pairs={{0,8},{8,16},{16,24},{1,9},{9,17},{17,25},{2,10},{10,18},{18,26},{... | collective-permute-start | bytes 1572872 | tf_op jit(solution)/shard_map/ppermute | solution.py:235
  138.8 10.7 %collective-permute-start.5 = (f32[8,128,128]{2,1,0:T(8,128)S(1)}, f32[8,128,128]{2,1,0:T(8,128)S(1)}, u32[]{:S(2)}, u32[]{:S(2)}) collective-permute-start(f32[8,128,128]{2,1,0:T(8,128)S(1)} %convolution_add_fusion), channel_id=1, source_target_pairs={{8,0},{16,8},{24,16},{9,1},{17,9},{25,17},{10,2},{18,10},{26,18},{... | collective-permute-start | bytes 1572872 | tf_op jit(solution)/shard_map/ppermute | solution.py:235
  149.4 62.5 %copy-start.1 = (bf16[1024,1024]{1,0:T(8,128)(2,1)S(1)}, bf16[1024,1024]{1,0:T(8,128)(2,1)}, u32[]{:S(2)}) copy-start(bf16[1024,1024]{1,0:T(8,128)(2,1)} %q_ref.3) | copy-start | bytes 6291460
  185.9 1.3 copy-start.2
  187.2 1.0 copy-start.4
  214.9 29.4 %copy-start.3 = (bf16[1024,1024]{1,0:T(8,128)(2,1)S(1)}, bf16[1024,1024]{1,0:T(8,128)(2,1)}, u32[]{:S(2)}) copy-start(bf16[1024,1024]{1,0:T(8,128)(2,1)} %copy-done.2) | copy-start | bytes 6291460
  274.1 28.0 %all-to-all-start.2 = ((bf16[8,128,1024]{2,1,0:T(8,128)(2,1)}), bf16[8,128,1024]{2,1,0:T(8,128)(2,1)S(1)}, u32[]{:S(2)}, u32[]{:S(2)}) async-start(bf16[8,128,1024]{2,1,0:T(8,128)(2,1)} %bitcast.38), calls=%async_computation.2 | async-start | bytes 4194304 | tf_op jit(solution)/shard_map/all_to_all | solution.py:359
  278.9 3.3 %copy-start.9 = (bf16[8,128,1024]{2,1,0:T(8,128)(2,1)S(1)}, bf16[8,128,1024]{2,1,0:T(8,128)(2,1)}, u32[]{:S(2)}) copy-start(bf16[8,128,1024]{2,1,0:T(8,128)(2,1)} %all_to_all.58) | copy-start | bytes 6291460

commit v2 on v1

--- a/solution.py
+++ b/solution.py
@@ -1,3 +1,4 @@
+import functools
 import math
 
 import jax
@@ -229,14 +230,216 @@
     corr_ref[0] = total
 
 
-def shift(value, axis, steps):
-    count = lax.axis_size(axis)
-    first, last = (max(0, -steps), min(count, count - steps))
-    return lax.ppermute(value, axis, [(i, i + steps) for i in range(first, last)])
-
-
-def apply_map(form, matrix, state):
-    return jnp.einsum(form, matrix, state, precision=lax.Precision.HIGHEST)
+def greet(axis, count):
+    me = lax.axis_index(axis)
+    barrier = pltpu.get_barrier_semaphore()
+    for offset in range(1, count):
+        pl.semaphore_signal(
+            barrier,
+            inc=1,
+            device_id={axis: lax.rem(me + offset, count)},
+            device_id_type=pl.DeviceIdType.MESH,
+        )
+    pl.semaphore_wait(barrier, count - 1)
+
+
+def remote(source, target, send, receive, axis, index):
+    return pltpu.make_async_remote_copy(
+        src_ref=source,
+        dst_ref=target,
+        send_sem=send,
+        recv_sem=receive,
+        device_id={axis: index},
+        device_id_type=pl.DeviceIdType.MESH,
+    )
+
+
+def share_rows(count, mine_ref, held_ref, send, receive):
+    me = lax.axis_index("head")
+    copies = [
+        remote(
+            mine_ref, held_ref.at[k], send.at[k], receive.at[k], "head", lax.rem(me + k, count)
+        )
+        for k in range(1, count)
+    ]
+    for copy in copies:
+        copy.start()
+    return copies
+
+
+def total_kernel(count, mine_ref, total_ref, held_ref, send, receive):
+    greet("head", count)
+    copies = share_rows(count, mine_ref, held_ref, send, receive)
+    for copy in copies:
+        copy.wait()
+    total = mine_ref[...]
+    for k in range(1, count):
+        total += held_ref[k]
+    total_ref[...] = total
+
+
+def states_kernel(
+    count, map_ref, adj_ref, in_ref, out_ref,
+    fsend, frecv, bsend, brecv, fsend_sem, frecv_sem, bsend_sem, brecv_sem,
+):
+    heads = adj_ref.shape[0]
+    me = lax.axis_index("seq")
+    first, last = me == 0, me == count - 1
+    barrier = pltpu.get_barrier_semaphore()
+    before, after = jnp.maximum(me - 1, 0), jnp.minimum(me + 1, count - 1)
+    mesh_id = pl.DeviceIdType.MESH
+
+    @pl.when(jnp.logical_not(first))
+    def _():
+        pl.semaphore_signal(barrier, inc=1, device_id={"seq": before}, device_id_type=mesh_id)
+
+    @pl.when(jnp.logical_not(last))
+    def _():
+        pl.semaphore_signal(barrier, inc=1, device_id={"seq": after}, device_id_type=mesh_id)
+
+    @pl.when(first | last)
+    def _():
+        pl.semaphore_wait(barrier, 1)
+
+    @pl.when(jnp.logical_not(first | last))
+    def _():
+        pl.semaphore_wait(barrier, 2)
+
+    def forward(h):
+        return remote(
+            fsend.at[h], frecv.at[h], fsend_sem.at[h], frecv_sem.at[h], "seq", after
+        )
+
+    def backward(h):
+        return remote(
+            bsend.at[h], brecv.at[h], bsend_sem.at[h], brecv_sem.at[h], "seq", before
+        )
+
+    def run(h, start, end, copy, recv, send, result, step):
+        @pl.when(start)
+        def _():
+            result[h] = jnp.zeros_like(result[h])
+            send[h] = step(h, None)
+
+        @pl.when(jnp.logical_not(start))
+        def _():
+            copy(h).wait_recv()
+            result[h] = recv[h]
+
+            @pl.when(jnp.logical_not(end))
+            def _():
+                send[h] = step(h, recv[h])
+
+        @pl.when(jnp.logical_not(end))
+        def _():
+            copy(h).start()
+
+    def forward_step(h, state):
+        offset = map_ref[h, :, BLOCK:]
+        return offset if state is None else prod(map_ref[h, :, :BLOCK], state) + offset
+
+    def backward_step(h, state):
+        offset = adj_ref[h]
+        return offset if state is None else prod(map_ref[h, :, :BLOCK], state, 0, 0) + offset
+
+    def turn(t, _):
+        h = t - me
+
+        @pl.when((h >= 0) & (h < heads))
+        def _():
+            run(h, first, last, forward, frecv, fsend, in_ref, forward_step)
+
+        k = t - (count - 1 - me)
+
+        @pl.when((k >= 0) & (k < heads))
+        def _():
+            run(k, last, first, backward, brecv, bsend, out_ref, backward_step)
+
+        return 0
+
+    lax.fori_loop(0, heads + count - 1, turn, 0)
+
+    @pl.when(jnp.logical_not(last))
+    def _():
+        for h in range(heads):
+            forward(h).wait_send()
+
+    @pl.when(jnp.logical_not(first))
+    def _():
+        for h in range(heads):
+            backward(h).wait_send()
+
+
+def finish_kernel(
+    count, full, scaled_hbm, query_hbm, key_hbm, value_hbm, inv_ref, corr_ref,
+    dq_hbm, dk_hbm, dv_hbm,
+    scaled, query, grad, held, load_sem, corr_send, corr_recv, send, receive, own_sem,
+):
+    me = lax.axis_index("head")
+    rows, width = scaled.shape
+    own = rows // count
+    blocks = rows // BLOCK
+    loads = [
+        pltpu.make_async_copy(scaled_hbm, scaled, load_sem.at[0]),
+        pltpu.make_async_copy(query_hbm, query, load_sem.at[1]),
+    ]
+    for load in loads:
+        load.start()
+    greet("head", count)
+    shares = share_rows(count, corr_ref, held, corr_send, corr_recv)
+    columns = pl.ds(pl.multiple_of(me * width, width), width)
+
+    def span(index):
+        return pl.ds(pl.multiple_of(index * own, own), own)
+
+    def sends(slot, source, target):
+        return [
+            remote(
+                source.at[span(lax.rem(me + k, count))],
+                target.at[:, columns],
+                send.at[slot, k],
+                receive.at[slot, k],
+                "head",
+                lax.rem(me + k, count),
+            )
+            for k in range(1, count)
+        ]
+
+    def keep(slot, source, target):
+        return pltpu.make_async_copy(
+            source.at[span(me)], target.at[:, columns], own_sem.at[slot]
+        )
+
+    key_sends = sends(1, key_hbm, dk_hbm)
+    value_sends = sends(2, value_hbm, dv_hbm)
+    query_sends = sends(0, grad, dq_hbm)
+    keeps = [keep(1, key_hbm, dk_hbm), keep(2, value_hbm, dv_hbm)]
+    for pair in zip(key_sends, value_sends):
+        for copy in pair:
+            copy.start()
+    for copy in keeps:
+        copy.start()
+    for load in loads:
+        load.wait()
+    for copy in shares:
+        copy.wait()
+    total = corr_ref[...]
+    for k in range(1, count):
+        total += held[k]
+    means = (total / full).T
+    for b in range(blocks):
+        part = slice(b * BLOCK, (b + 1) * BLOCK)
+        inv = inv_ref[:, b : b + 1]
+        normed = query[part, :].astype(jnp.float32) * inv
+        grad[part, :] = (inv * (scaled[part, :] - normed * means[:, b : b + 1])).astype(
+            jnp.bfloat16
+        )
+    last = keep(0, grad, dq_hbm)
+    last.start()
+    for copy in query_sends:
+        copy.start()
+    for copy in keeps + [last] + key_sends + value_sends + query_sends:
+        copy.wait()
 
 
 def per_device(query_raw, key_raw, value_raw, query_gain, log_decay, out_grad):
@@ -250,8 +453,23 @@
     f32 = jnp.float32
 
     raw_query = query_raw.astype(f32)
-    squares = lax.psum(jnp.sum(raw_query * raw_query, axis=1), "head")
-    inv = lax.rsqrt(squares / full + epsilon)[:, None]
+    count = lax.axis_size("head")
+    turns = lax.axis_size("seq")
+    dma = pltpu.SemaphoreType.DMA
+    in_vmem = pl.BlockSpec(memory_space=pltpu.VMEM)
+    anywhere = pl.BlockSpec(memory_space=pl.ANY)
+    row_shape = jax.ShapeDtypeStruct((blocks, BLOCK), f32)
+    squares = pl.pallas_call(
+        functools.partial(total_kernel, count),
+        in_specs=[in_vmem],
+        out_specs=in_vmem,
+        out_shape=row_shape,
+        scratch_shapes=[pltpu.VMEM((count, blocks, BLOCK), f32), dma((count,)), dma((count,))],
+        compiler_params=pltpu.CompilerParams(collective_id=0, has_side_effects=True),
+        name="token_squares",
+    )(jnp.sum((raw_query * raw_query).reshape(blocks, BLOCK, width), axis=2))
+    inv_rows = lax.rsqrt(squares / full + epsilon)
+    inv = inv_rows.reshape(rows, 1)
     gain = query_gain * size ** (-0.5)
     gain_row = gain[None, :]
     gain_col = gain.reshape(heads, size, 1)
@@ -317,16 +535,18 @@
         query_raw, key_raw, out_grad, crow, ccol, inv, gain_row, gain_col, weight, trans, offset
     )
 
-    through, shifted = device_map[:, :, :size], device_map[:, :, size:]
-    incoming = jnp.zeros((heads, size, size), f32)
-    outgoing = jnp.zeros((heads, size, size), f32)
-    for step in range(lax.axis_size("seq") - 1):
-        ahead, back = shifted, device_adjoint
-        if step:
-            ahead = apply_map("hij,hjk->hik", through, incoming) + ahead
-            back = apply_map("hji,hjk->hik", through, outgoing) + back
-        incoming = shift(ahead, "seq", 1)
-        outgoing = shift(back, "seq", -1)
+    state = jax.ShapeDtypeStruct((heads, size, size), f32)
+    incoming, outgoing = pl.pallas_call(
+        functools.partial(states_kernel, turns),
+        in_specs=[in_vmem, in_vmem],
+        out_specs=[in_vmem, in_vmem],
+        out_shape=[state, state],
+        scratch_shapes=[pltpu.VMEM((heads, size, size), f32)] * 4 + [dma((heads,))] * 4,
+        compiler_params=pltpu.CompilerParams(
+            collective_id=1, has_side_effects=True, vmem_limit_bytes=VMEM
+        ),
+        name="device_states",
+    )(device_map, device_adjoint)
 
     s = specs(lambda b: blocks - 1 - b)
     scaled, key_grad, value_grad, correction = pl.pallas_call(
@@ -352,13 +572,32 @@
         inverse, weight, initial, trans, adjoint, inner, prefix, incoming, outgoing,
     )
 
-    correction = lax.psum(jnp.sum(correction, axis=0), "head") / full
-    query_grad = (inv * (scaled - raw_query * inv * correction)).astype(jnp.bfloat16)
-
-    def to_owner(array):
-        return lax.all_to_all(array, "head", split_axis=0, concat_axis=1, tiled=True)
-
-    return to_owner(query_grad), to_owner(key_grad), to_owner(value_grad)
+    owned = jax.ShapeDtypeStruct((rows // count, full), jnp.bfloat16)
+    return pl.pallas_call(
+        functools.partial(finish_kernel, count, full),
+        in_specs=[anywhere] * 4 + [in_vmem] * 2,
+        out_specs=[anywhere] * 3,
+        out_shape=[owned] * 3,
+        scratch_shapes=[
+            pltpu.VMEM((rows, width), f32),
+            pltpu.VMEM((rows, width), jnp.bfloat16),
+            pltpu.VMEM((rows, width), jnp.bfloat16),
+            pltpu.VMEM((count, blocks, BLOCK), f32),
+            dma((2,)),
+            dma((count,)),
+            dma((count,)),
+            dma((3, count)),
+            dma((3, count)),
+            dma((3,)),
+        ],
+        compiler_params=pltpu.CompilerParams(
+            collective_id=2, has_side_effects=True, vmem_limit_bytes=VMEM
+        ),
+        name="send_gradients",
+    )(
+        scaled, query_raw, key_grad, value_grad, inv_rows.T,
+        jnp.sum(correction, axis=0).reshape(blocks, BLOCK),
+    )
 
 
 def solution(mesh):

time: 308 us -> 256 us (0.83); the launches traced: 304 us -> 255 us
  Pallas kernels: 122 us -> 235 us
  blocking collectives: 94 us -> 0 us
  waiting for transfers between devices: 40.5 us -> 0 us
  starting transfers between devices: 20.4 us -> 0 us
  other arithmetic: 9.47 us -> 4.23 us
  matrix products: 3.4 us -> 0 us
    pallas_call x0 -> x3, Pallas kernels: none -> 114 us  [the longest x1 80.2 us: per_device(): pl.pallas_call(functools.partial(finish_kernel, count, full), in_specs=[a...]
    all_to_all x2 -> x0, blocking collectives: 59.1 us -> none  [to_owner(): lax.all_to_all(array, 'head', split_axis=0, concat_axis=1, tiled=True)]
    psum x2 -> x0, blocking collectives: 34.8 us -> none  [the longest x1 22.3 us: per_device(): correction = lax.psum(jnp.sum(correction, axis=0), 'head') / full]
    ppermute x6 -> x0, waiting for transfers between devices: 22.2 us -> none  [shift(): lax.ppermute(value, axis, [(i, i + steps) for i in range(first, last)])]
    all_to_all x1 -> x0, waiting for transfers between devices: 18.3 us -> none  [to_owner(): lax.all_to_all(array, 'head', split_axis=0, concat_axis=1, tiled=True)]
    ppermute x6 -> x0, starting transfers between devices: 15.6 us -> none  [shift(): lax.ppermute(value, axis, [(i, i + steps) for i in range(first, last)])]
    all_to_all x3 -> x0, local copies, waits for them, and re-layouts: 6.35 us -> none  [to_owner(): lax.all_to_all(array, 'head', split_axis=0, concat_axis=1, tiled=True)]
    unnamed x20 -> x21, local copies, waits for them, and re-layouts: 5.49 us -> 11.6 us
  transfers between devices with their start and end apart: 7 -> 0, of which waited for: 6 -> 0; matrix products, arithmetic and copies ran while one was open for 3% -> 0% of each run, Pallas kernels for 0% -> 0%
where the time goes in v2:
time: 256 us; the launch traced here: 255 us
  Pallas kernels  235 us (92%)
  local copies, waits for them, and re-layouts  14.9 us (6%)
  other arithmetic  4.23 us (2%)
    pallas_call x1, Pallas kernels, per_device(): pl.pallas_call(functools.partial(finish_kernel, count, full), in_specs=[a...  80.2 us
    pallas_call x1, Pallas kernels, per_device(): pl.pallas_call(maps_kernel, grid=grid, in_specs=[s['raw'], s['raw'], s['c...  52.2 us
    pallas_call x1, Pallas kernels, per_device(): pl.pallas_call(grads_kernel, grid=grid, in_specs=[s['raw']] * 3 + [s['cro...  36.1 us
    pallas_call x1, Pallas kernels, per_device(): pl.pallas_call(chain_kernel, grid=grid, in_specs=[s['raw']] * 3 + [s['cro...  32.6 us
    pallas_call x1, Pallas kernels, per_device(): pl.pallas_call(functools.partial(states_kernel, turns), in_specs=[in_vmem...  27 us
    unnamed x21, local copies, waits for them, and re-layouts  11.6 us
    pallas_call x1, Pallas kernels, per_device(): pl.pallas_call(functools.partial(total_kernel, count), in_specs=[in_vmem]...  7.23 us

profile of v2, /device:TPU:1, one launch (start us, length us, event | category | flops | bytes accessed | tf_op | source)
XLA Modules:
  0.0 255.2 jit_solution(14033503157555255679)
XLA Ops:
  0.6 0.8 copy.22
  1.4 2.3 reduce_window_sum.11
  3.7 0.4 copy.23
  4.1 1.6 copy-done.5
  5.6 1.6 copy-done.6
  7.2 52.2 %block_maps.1 = (f32[8,8,128,128]{3,2,1,0:T(8,128)}, f32[8,8,128,128]{3,2,1,0:T(8,128)}, f32[8,8,128,128]{3,2,1,0:T(8,128)}, f32[8,8,128,128]{3,2,1,0:T(8,128)}, f32[8,8,128,128]{3,2,1,0:T(8,128)}) custom-call(bf16[1024,1024]{1,0:T(8,128)(2,1)S(1)} %copy-done.6, bf16[1024,1024]{1,0:T(8,128)(2,1)S(1)} %copy-done.5, f32[8,1,1024]{2,1,0:T(1,128)S(1)} %bitcast.14, ...), custom_call_target="tpu_custom_call" | custom-call | flops 42949672960 | bytes 25165824 | tf_op jit(solution)/shard_map/block_maps/pallas_call | solution.py:507
  59.5 1.1 multiply_reduce_fusion
  60.5 7.2 %token_squares.1 = f32[8,128]{1,0:T(8,128)} custom-call(f32[8,128]{1,0:T(8,128)} %bitcast.22), custom_call_target="tpu_custom_call" | custom-call | tf_op jit(solution)/shard_map/token_squares/pallas_call | solution.py:462
  67.8 0.7 add_rsqrt_fusion
  68.5 1.0 copy.26.inv_ref
  69.5 1.0 copy.25.gcol_ref
  70.5 1.0 copy-done.2
  71.6 1.0 copy-done.4
  72.6 32.6 %device_maps.1 = (f32[8,8,128,128]{3,2,1,0:T(8,128)}, f32[8,8,128,128]{3,2,1,0:T(8,128)}, f32[8,8,128,256]{3,2,1,0:T(8,128)}, f32[8,128,256]{2,1,0:T(8,128)S(1)}, f32[8,128,128]{2,1,0:T(8,128)S(1)}) custom-call(bf16[1024,1024]{1,0:T(8,128)(2,1)S(1)} %copy-done, bf16[1024,1024]{1,0:T(8,128)(2,1)} %k_ref.5, bf16[1024,1024]{1,0:T(8,128)(2,1)} %g_ref.3, ...), custom_call_target="tpu_custom_call" | custom-call | flops 21474836480 | bytes 25165824 | tf_op jit(solution)/shard_map/device_maps/pallas_call | solution.py:517
  105.2 27.0 %device_states.1 = (f32[8,128,128]{2,1,0:T(8,128)S(1)}, f32[8,128,128]{2,1,0:T(8,128)S(1)}) custom-call(f32[8,128,256]{2,1,0:T(8,128)S(1)} %get-tuple-element.27.map_ref, f32[8,128,128]{2,1,0:T(8,128)S(1)} %get-tuple-element.28.adj_ref), custom_call_target="tpu_custom_call" | custom-call | tf_op jit(solution)/shard_map/device_states/pallas_call | solution.py:539
  132.3 36.1 %block_grads.1 = (f32[1024,1024]{1,0:T(8,128)}, bf16[1024,1024]{1,0:T(8,128)(2,1)S(1)}, bf16[1024,1024]{1,0:T(8,128)(2,1)}, f32[2,1024,1]{2,1,0:T(8,128)S(1)}) custom-call(bf16[1024,1024]{1,0:T(8,128)(2,1)} %query_hbm.1, bf16[1024,1024]{1,0:T(8,128)(2,1)} %k_ref.5, bf16[1024,1024]{1,0:T(8,128)(2,1)} %g_ref.3, f32[8,1,1024]{2,1,0:T(1,128)S(1)} %bitcast.16, ...), custom_call_target="tpu_custom_call" | custom-call | flops 42949672960 | bytes 25165824 | tf_op jit(solution)/shard_map/block_grads/pallas_call | solution.py:552
  168.4 1.3 copy-done.1
  169.7 0.2 reduce_sum.22
  169.9 0.1 copy.27
  170.0 80.2 %send_gradients.1 = (bf16[128,8192]{1,0:T(8,128)(2,1)S(1)}, bf16[128,8192]{1,0:T(8,128)(2,1)S(1)}, bf16[128,8192]{1,0:T(8,128)(2,1)}) custom-call(f32[1024,1024]{1,0:T(8,128)} %get-tuple-element.31.scaled_hbm, bf16[1024,1024]{1,0:T(8,128)(2,1)} %query_hbm.1, bf16[1024,1024]{1,0:T(8,128)(2,1)} %copy-done.1, bf16[1024,1024]{1,0:T(8,128)(2,1)} %get-tuple-element.33.value_hbm, ...), custom_call_target="tpu_custom_call" | custom-call | tf_op jit(solution)/shard_map/send_gradients/pallas_call | solution.py:576
  250.2 1.3 copy.31
  251.5 1.3 copy.32
  252.8 1.0 copy-done.7
  253.9 1.3 copy.33
  (14 shorter events, 0.0 us)
Async XLA Ops:
  4.0 1.6 copy-start.5
  5.6 1.6 copy-start.6
  7.2 52.2 %copy-start = (bf16[1024,1024]{1,0:T(8,128)(2,1)S(1)}, bf16[1024,1024]{1,0:T(8,128)(2,1)}, u32[]{:S(2)}) copy-start(bf16[1024,1024]{1,0:T(8,128)(2,1)} %query_hbm.1) | copy-start | bytes 6291460
  59.5 10.0 %copy-start.8 = (f32[1024]{0:T(1024)S(1)}, f32[1024]{0:T(1024)}, u32[]{:S(2)}) copy-start(f32[1024]{0:T(1024)} %param.9) | copy-start | bytes 12292
  70.5 1.0 copy-start.2
  71.6 1.0 copy-start.4
  72.6 59.6 %copy-start.3 = (f32[1024,1]{1,0:T(8,128)S(1)}, f32[1024,1]{1,0:T(8,128)}, u32[]{:S(2)}) copy-start(f32[1024,1]{1,0:T(8,128)} %copy.26.inv_ref) | copy-start | bytes 12292
  168.4 1.3 copy-start.1
  251.5 2.3 copy-start.7

commit v3 on v2

--- a/solution.py
+++ b/solution.py
@@ -9,6 +9,7 @@
 from jax.sharding import PartitionSpec as P
 
 BLOCK = 128
+WIDE = 8
 GROUP = 4
 VMEM = 48 * 1024 * 1024
 
@@ -96,12 +97,29 @@
         across = (row // size) != (column // size)
         return jnp.where(inside & across, x, 0.0)
 
+    def second(x, size):
+        return jnp.concatenate(
+            [x[i + size : i + 2 * size] for i in range(0, BLOCK, 2 * size)], axis=0
+        )
+
+    def spread(x, size):
+        zeros = jnp.zeros((size, BLOCK), x.dtype)
+        pieces = []
+        for i in range(0, BLOCK // 2, size):
+            pieces += [zeros, x[i : i + size]]
+        return jnp.concatenate(pieces, axis=0)
+
     inverse = [eye - pick(x, 1) for x in lower]
     size = 2
     while size < BLOCK:
         split = [parts(x) for x in inverse]
-        inner = [prod(pick(x, size), s) for x, s in zip(lower, split)]
-        inverse = [t - prod(s, y) for t, s, y in zip(inverse, split, inner)]
+        if size < 8:
+            inner = [prod(pick(x, size), p) for x, p in zip(lower, split)]
+            inverse = [t - prod(p, y) for t, p, y in zip(inverse, split, inner)]
+        else:
+            inner = [prod(second(pick(x, size), size), p) for x, p in zip(lower, split)]
+            change = [prod(second(t, size), spread(y, size)) for t, y in zip(inverse, inner)]
+            inverse = [t - spread(y, size) for t, y in zip(inverse, change)]
         size *= 2
     for h in range(group):
         t_ref[h, 0] = inverse[h]
@@ -447,8 +465,6 @@
     heads = log_decay.shape[0]
     size = width // heads
     blocks = rows // BLOCK
-    group = math.gcd(heads, GROUP)
-    groups = heads // group
     full = width * lax.axis_size("head")
     f32 = jnp.float32
 
@@ -475,9 +491,11 @@
     gain_col = gain.reshape(heads, size, 1)
     cumul = jnp.cumsum(log_decay.reshape(heads, blocks, BLOCK), axis=2).reshape(heads, rows)
     crow = cumul[:, None, :]
-    ccol = cumul.reshape(groups, group, rows).transpose(0, 2, 1)
-
-    def specs(order):
+
+    def columns_of(group):
+        return cumul.reshape(heads // group, group, rows).transpose(0, 2, 1)
+
+    def specs(group, order):
         return dict(
             raw=pl.BlockSpec((BLOCK, group * size), lambda g, b: (order(b), g)),
             crow=pl.BlockSpec((group, 1, BLOCK), lambda g, b: (g, 0, order(b))),
@@ -492,7 +510,6 @@
             corr=pl.BlockSpec((1, BLOCK, 1), lambda g, b: (g, order(b), 0)),
         )
 
-    grid = (groups, blocks)
     mat = jax.ShapeDtypeStruct((heads, blocks, size, size), f32)
     pre = jax.ShapeDtypeStruct((heads, blocks, size, 2 * size), f32)
     params = pltpu.CompilerParams(
@@ -503,7 +520,10 @@
         flops = 2 * passes * BLOCK**3 * heads * blocks
         return pl.CostEstimate(flops=flops, bytes_accessed=24 * 2**20, transcendentals=0)
 
-    s = specs(lambda b: b)
+    group = math.gcd(heads, WIDE)
+    grid = (heads // group, blocks)
+    ccol = columns_of(group)
+    s = specs(group, lambda b: b)
     inverse, weight, initial, trans, offset = pl.pallas_call(
         maps_kernel,
         grid=grid,
@@ -548,7 +568,11 @@
         name="device_states",
     )(device_map, device_adjoint)
 
-    s = specs(lambda b: blocks - 1 - b)
+    group = math.gcd(heads, GROUP)
+    groups = heads // group
+    grid = (groups, blocks)
+    ccol = columns_of(group)
+    s = specs(group, lambda b: blocks - 1 - b)
     scaled, key_grad, value_grad, correction = pl.pallas_call(
         grads_kernel,
         grid=grid,

time: 256 us -> 221 us (0.86)
  Pallas kernels: 235 us -> 200 us
    pallas_call x1, Pallas kernels: 52.2 us -> 28.9 us  [per_device(): pl.pallas_call(maps_kernel, grid=grid, in_specs=[s['raw'], s['raw'], s['c...]
    pallas_call x1, Pallas kernels: 32.6 us -> 20.8 us  [per_device(): pl.pallas_call(chain_kernel, grid=grid, in_specs=[s['raw']] * 3 + [s['cro...]
where the time goes in v3:
time: 221 us; the launch traced here: 220 us
  Pallas kernels  200 us (90%)
  local copies, waits for them, and re-layouts  15.1 us (7%)
  other arithmetic  4.23 us (2%)
    pallas_call x1, Pallas kernels, per_device(): pl.pallas_call(functools.partial(finish_kernel, count, full), in_specs=[a...  80.1 us
    pallas_call x1, Pallas kernels, per_device(): pl.pallas_call(grads_kernel, grid=grid, in_specs=[s['raw']] * 3 + [s['cro...  36.3 us
    pallas_call x1, Pallas kernels, per_device(): pl.pallas_call(maps_kernel, grid=grid, in_specs=[s['raw'], s['raw'], s['c...  28.9 us
    pallas_call x1, Pallas kernels, per_device(): pl.pallas_call(functools.partial(states_kernel, turns), in_specs=[in_vmem...  27 us
    pallas_call x1, Pallas kernels, per_device(): pl.pallas_call(chain_kernel, grid=grid, in_specs=[s['raw']] * 3 + [s['cro...  20.8 us
    unnamed x21, local copies, waits for them, and re-layouts  12.4 us
    pallas_call x1, Pallas kernels, per_device(): pl.pallas_call(functools.partial(total_kernel, count), in_specs=[in_vmem]...  7.23 us

profile of v3, /device:TPU:1, one launch (start us, length us, event | category | flops | bytes accessed | tf_op | source)
XLA Modules:
  0.0 220.4 jit_solution(3702586200635767551)
XLA Ops:
  0.6 0.8 copy.24
  1.4 2.3 %reduce_window_sum.11 = f32[8,8,128]{2,1,0:T(8,128)S(1)} reduce-window(f32[8,8,128]{2,1,0:T(8,128)S(1)} %copy.24, f32[]{:T(128)} %constant.4.clone.1), window={size=1x1x128 pad=0_0x0_0x127_0}, to_apply=%region_0.0 | reduce-window | flops 1040384 | bytes 65540 | tf_op jit(solution)/shard_map/jit(cumsum)/reduce_window_sum | solution.py:492
  3.9 1.6 copy-done.3
  5.5 1.6 copy-done.4
  7.1 28.9 %block_maps.1 = (f32[8,8,128,128]{3,2,1,0:T(8,128)}, f32[8,8,128,128]{3,2,1,0:T(8,128)}, f32[8,8,128,128]{3,2,1,0:T(8,128)}, f32[8,8,128,128]{3,2,1,0:T(8,128)}, f32[8,8,128,128]{3,2,1,0:T(8,128)}) custom-call(bf16[1024,1024]{1,0:T(8,128)(2,1)S(1)} %copy-done.4, bf16[1024,1024]{1,0:T(8,128)(2,1)S(1)} %copy-done.3, f32[8,1,1024]{2,1,0:T(1,128)S(1)} %bitcast.16, ...), custom_call_target="tpu_custom_call" | custom-call | flops 42949672960 | bytes 25165824 | tf_op jit(solution)/shard_map/block_maps/pallas_call | solution.py:527
  35.9 1.1 multiply_reduce_fusion
  37.0 7.2 %token_squares.1 = f32[8,128]{1,0:T(8,128)} custom-call(f32[8,128]{1,0:T(8,128)} %bitcast.25), custom_call_target="tpu_custom_call" | custom-call | tf_op jit(solution)/shard_map/token_squares/pallas_call | solution.py:478
  44.2 0.7 add_rsqrt_fusion
  44.9 0.2 copy.29.inv_ref
  45.2 1.0 copy.28.gcol_ref
  46.2 1.0 copy-done.2
  47.2 20.8 %device_maps.1 = (f32[8,8,128,128]{3,2,1,0:T(8,128)}, f32[8,8,128,128]{3,2,1,0:T(8,128)}, f32[8,8,128,256]{3,2,1,0:T(8,128)}, f32[8,128,256]{2,1,0:T(8,128)S(1)}, f32[8,128,128]{2,1,0:T(8,128)S(1)}) custom-call(bf16[1024,1024]{1,0:T(8,128)(2,1)S(1)} %copy-done, bf16[1024,1024]{1,0:T(8,128)(2,1)} %k_ref.5, bf16[1024,1024]{1,0:T(8,128)(2,1)} %g_ref.3, ...), custom_call_target="tpu_custom_call" | custom-call | flops 21474836480 | bytes 25165824 | tf_op jit(solution)/shard_map/device_maps/pallas_call | solution.py:537
  68.0 27.0 %device_states.1 = (f32[8,128,128]{2,1,0:T(8,128)S(1)}, f32[8,128,128]{2,1,0:T(8,128)S(1)}) custom-call(f32[8,128,256]{2,1,0:T(8,128)S(1)} %get-tuple-element.27.map_ref, f32[8,128,128]{2,1,0:T(8,128)S(1)} %get-tuple-element.28.adj_ref), custom_call_target="tpu_custom_call" | custom-call | tf_op jit(solution)/shard_map/device_states/pallas_call | solution.py:559
  95.1 0.8 copy-done.5
  95.9 0.4 copy.25
  96.2 1.0 copy-done.6
  97.3 36.3 %block_grads.1 = (f32[1024,1024]{1,0:T(8,128)}, bf16[1024,1024]{1,0:T(8,128)(2,1)S(1)}, bf16[1024,1024]{1,0:T(8,128)(2,1)}, f32[2,1024,1]{2,1,0:T(8,128)S(1)}) custom-call(bf16[1024,1024]{1,0:T(8,128)(2,1)} %query_hbm.1, bf16[1024,1024]{1,0:T(8,128)(2,1)} %k_ref.5, bf16[1024,1024]{1,0:T(8,128)(2,1)} %g_ref.3, f32[8,1,1024]{2,1,0:T(1,128)S(1)} %bitcast.18, ...), custom_call_target="tpu_custom_call" | custom-call | flops 42949672960 | bytes 25165824 | tf_op jit(solution)/shard_map/block_grads/pallas_call | solution.py:576
  133.6 1.3 copy-done.1
  135.0 0.2 reduce_sum.22
  135.3 80.1 %send_gradients.1 = (bf16[128,8192]{1,0:T(8,128)(2,1)S(1)}, bf16[128,8192]{1,0:T(8,128)(2,1)S(1)}, bf16[128,8192]{1,0:T(8,128)(2,1)}) custom-call(f32[1024,1024]{1,0:T(8,128)} %get-tuple-element.31.scaled_hbm, bf16[1024,1024]{1,0:T(8,128)(2,1)} %query_hbm.1, bf16[1024,1024]{1,0:T(8,128)(2,1)} %copy-done.1, bf16[1024,1024]{1,0:T(8,128)(2,1)} %get-tuple-element.33.value_hbm, ...), custom_call_target="tpu_custom_call" | custom-call | tf_op jit(solution)/shard_map/send_gradients/pallas_call | solution.py:600
  215.4 1.3 copy.34
  216.7 1.3 copy.35
  218.1 1.0 copy-done.7
  219.1 1.3 copy.36
  (15 shorter events, 0.4 us)
Async XLA Ops:
  3.9 1.6 copy-start.3
  5.5 1.6 copy-start.4
  7.1 28.9 %copy-start = (bf16[1024,1024]{1,0:T(8,128)(2,1)S(1)}, bf16[1024,1024]{1,0:T(8,128)(2,1)}, u32[]{:S(2)}) copy-start(bf16[1024,1024]{1,0:T(8,128)(2,1)} %query_hbm.1) | copy-start | bytes 6291460
  35.9 9.2 %copy-start.8 = (f32[1024]{0:T(1024)S(1)}, f32[1024]{0:T(1024)}, u32[]{:S(2)}) copy-start(f32[1024]{0:T(1024)} %param.9) | copy-start | bytes 12292
  46.2 1.0 copy-start.2
  95.1 0.8 copy-start.5
  96.2 1.0 copy-start.6
  133.6 1.3 copy-start.1
  216.7 2.3 %copy-start.7 = (bf16[128,8192]{1,0:T(8,128)(2,1)S(1)}, bf16[128,8192]{1,0:T(8,128)(2,1)}, u32[]{:S(2)}) copy-start(bf16[128,8192]{1,0:T(8,128)(2,1)} %get-tuple-element.42) | copy-start | bytes 6291460

commit v4 on v3

--- a/solution.py
+++ b/solution.py
@@ -184,17 +184,33 @@
 
 
 def grads_kernel(
+    count, full,
     q_ref, k_ref, g_ref, crow_ref, ccol_ref, inv_ref, gain_ref,
     t_ref, w_ref, u_ref, a_ref, c_ref, inner_ref, pre_ref, in_ref, out_ref,
-    dq_ref, dk_ref, dv_ref, corr_ref, carry_ref,
+    inv_cols, dq_hbm, dk_hbm, dv_hbm,
+    carry_ref, scaled, query, grad, dkeys, dvalues, corr, held,
+    corr_send, corr_recv, query_send, query_recv, send, receive, own_sem,
 ):
     group = crow_ref.shape[0]
     heads = range(group)
     row, column = slots()
-
-    @pl.when(pl.program_id(1) == 0)
+    turn, step = pl.program_id(0), pl.program_id(1)
+    turns, blocks, span_width = scaled.shape[0], corr.shape[0], group * BLOCK
+    rows = scaled.shape[1]
+    own = rows // count
+    width = turns * span_width
+    me = lax.axis_index("head")
+    block = blocks - 1 - step
+    place = pl.ds(pl.multiple_of(block * BLOCK, BLOCK), BLOCK)
+
+    @pl.when(step == 0)
     def _():
         carry_ref[...] = out_ref[...]
+
+    @pl.when((step == 0) & (turn == 0))
+    def _():
+        greet("head", count)
+        corr[...] = jnp.zeros_like(corr)
 
     queries = lanes(q_ref, group)
     keys = lanes(k_ref, group)
@@ -235,17 +251,82 @@
         dkey[h] + gains[h] * prod(spread[h] * inv, queries[h], 0, 0) for h in heads
     ]
     total = jnp.zeros((BLOCK, 1), jnp.float32)
+    query[turn, place, :] = q_ref[...]
     for h in heads:
         span = slice(h * BLOCK, (h + 1) * BLOCK)
-        scaled = dquery[h] * gains[h]
-        dq_ref[:, span] = scaled
-        total += jnp.sum(scaled * (queries[h].astype(jnp.float32) * inv), axis=1, keepdims=True)
-        dv_ref[:, span] = target[h].astype(jnp.bfloat16)
+        gradient = dquery[h] * gains[h]
+        scaled[turn, place, span] = gradient
+        total += jnp.sum(gradient * (queries[h].astype(jnp.float32) * inv), axis=1, keepdims=True)
+        dvalues[turn, place, span] = target[h].astype(jnp.bfloat16)
         scale = scales[h][1]
         unit = keys[h].astype(jnp.float32) * scale
         along = jnp.sum(unit * dkey[h], axis=1, keepdims=True)
-        dk_ref[:, span] = (scale * (dkey[h] - unit * along)).astype(jnp.bfloat16)
-    corr_ref[0] = total
+        dkeys[turn, place, span] = (scale * (dkey[h] - unit * along)).astype(jnp.bfloat16)
+    corr[pl.ds(block, 1), :] += jnp.sum(jnp.where(row == column, total, 0.0), axis=0, keepdims=True)
+
+    def owned(index):
+        return pl.ds(pl.multiple_of(index * own, own), own)
+
+    def columns(g):
+        return pl.ds(pl.multiple_of(me * width + g * span_width, span_width), span_width)
+
+    def moves(source, target, g, out_sem, in_sem, kept_sem):
+        kept = pltpu.make_async_copy(
+            source.at[g, owned(me)], target.at[:, columns(g)], kept_sem
+        )
+        sent = [
+            remote(
+                source.at[g, owned(lax.rem(me + k, count))],
+                target.at[:, columns(g)],
+                out_sem.at[g, k],
+                in_sem.at[g, k],
+                "head",
+                lax.rem(me + k, count),
+            )
+            for k in range(1, count)
+        ]
+        return [kept] + sent
+
+    def key_moves(g):
+        return moves(dkeys, dk_hbm, g, send.at[0], receive.at[0], own_sem.at[0, g])
+
+    def value_moves(g):
+        return moves(dvalues, dv_hbm, g, send.at[1], receive.at[1], own_sem.at[1, g])
+
+    def query_moves(g):
+        return moves(grad, dq_hbm, g, query_send, query_recv, own_sem.at[2, g])
+
+    @pl.when((step == blocks - 1) & (turn < turns - 1))
+    def _():
+        for pair in zip(key_moves(turn), value_moves(turn)):
+            for copy in pair:
+                copy.start()
+
+    @pl.when((step == blocks - 1) & (turn == turns - 1))
+    def _():
+        shares = share_rows(count, corr, held, corr_send, corr_recv)
+        for pair in zip(key_moves(turns - 1), value_moves(turns - 1)):
+            for copy in pair:
+                copy.start()
+        for copy in shares:
+            copy.wait()
+        summed = corr[...]
+        for k in range(1, count):
+            summed += held[k]
+        means = (summed / full).T
+        for g in range(turns):
+            for b in range(blocks):
+                part = slice(b * BLOCK, (b + 1) * BLOCK)
+                inverse = inv_cols[:, b : b + 1]
+                normed = query[g, part, :].astype(jnp.float32) * inverse
+                grad[g, part, :] = (
+                    inverse * (scaled[g, part, :] - normed * means[:, b : b + 1])
+                ).astype(jnp.bfloat16)
+            for copy in query_moves(g):
+                copy.start()
+        for g in range(turns):
+            for copy in key_moves(g) + value_moves(g) + query_moves(g):
+                copy.wait()
 
 
 def greet(axis, count):
@@ -386,78 +467,6 @@
     def _():
         for h in range(heads):
             backward(h).wait_send()
-
-
-def finish_kernel(
-    count, full, scaled_hbm, query_hbm, key_hbm, value_hbm, inv_ref, corr_ref,
-    dq_hbm, dk_hbm, dv_hbm,
-    scaled, query, grad, held, load_sem, corr_send, corr_recv, send, receive, own_sem,
-):
-    me = lax.axis_index("head")
-    rows, width = scaled.shape
-    own = rows // count
-    blocks = rows // BLOCK
-    loads = [
-        pltpu.make_async_copy(scaled_hbm, scaled, load_sem.at[0]),
-        pltpu.make_async_copy(query_hbm, query, load_sem.at[1]),
-    ]
-    for load in loads:
-        load.start()
-    greet("head", count)
-    shares = share_rows(count, corr_ref, held, corr_send, corr_recv)
-    columns = pl.ds(pl.multiple_of(me * width, width), width)
-
-    def span(index):
-        return pl.ds(pl.multiple_of(index * own, own), own)
-
-    def sends(slot, source, target):
-        return [
-            remote(
-                source.at[span(lax.rem(me + k, count))],
-                target.at[:, columns],
-                send.at[slot, k],
-                receive.at[slot, k],
-                "head",
-                lax.rem(me + k, count),
-            )
-            for k in range(1, count)
-        ]
-
-    def keep(slot, source, target):
-        return pltpu.make_async_copy(
-            source.at[span(me)], target.at[:, columns], own_sem.at[slot]
-        )
-
-    key_sends = sends(1, key_hbm, dk_hbm)
-    value_sends = sends(2, value_hbm, dv_hbm)
-    query_sends = sends(0, grad, dq_hbm)
-    keeps = [keep(1, key_hbm, dk_hbm), keep(2, value_hbm, dv_hbm)]
-    for pair in zip(key_sends, value_sends):
-        for copy in pair:
-            copy.start()
-    for copy in keeps:
-        copy.start()
-    for load in loads:
-        load.wait()
-    for copy in shares:
-        copy.wait()
-    total = corr_ref[...]
-    for k in range(1, count):
-        total += held[k]
-    means = (total / full).T
-    for b in range(blocks):
-        part = slice(b * BLOCK, (b + 1) * BLOCK)
-        inv = inv_ref[:, b : b + 1]
-        normed = query[part, :].astype(jnp.float32) * inv
-        grad[part, :] = (inv * (scaled[part, :] - normed * means[:, b : b + 1])).astype(
-            jnp.bfloat16
-        )
-    last = keep(0, grad, dq_hbm)
-    last.start()
-    for copy in query_sends:
-        copy.start()
-    for copy in keeps + [last] + key_sends + value_sends + query_sends:
-        copy.wait()
 
 
 def per_device(query_raw, key_raw, value_raw, query_gain, log_decay, out_grad):
@@ -573,54 +582,46 @@
     grid = (groups, blocks)
     ccol = columns_of(group)
     s = specs(group, lambda b: blocks - 1 - b)
-    scaled, key_grad, value_grad, correction = pl.pallas_call(
-        grads_kernel,
+    owned = jax.ShapeDtypeStruct((rows // count, full), jnp.bfloat16)
+    span = group * size
+    half = pltpu.VMEM((groups, rows, span), jnp.bfloat16)
+    return pl.pallas_call(
+        functools.partial(grads_kernel, count, full),
         grid=grid,
         in_specs=[s["raw"]] * 3
         + [s["crow"], s["ccol"], s["inv"], s["gain"]]
         + [s["mat"]] * 6
-        + [s["pre"], s["head"], s["head"]],
-        out_specs=[s["raw"], s["raw"], s["raw"], s["corr"]],
-        out_shape=[
-            jax.ShapeDtypeStruct((rows, width), f32),
-            jax.ShapeDtypeStruct((rows, width), jnp.bfloat16),
-            jax.ShapeDtypeStruct((rows, width), jnp.bfloat16),
-            jax.ShapeDtypeStruct((groups, rows, 1), f32),
+        + [s["pre"], s["head"], s["head"], pl.BlockSpec((BLOCK, blocks), lambda g, b: (0, 0))],
+        out_specs=[anywhere] * 3,
+        out_shape=[owned] * 3,
+        scratch_shapes=[
+            pltpu.VMEM((group, size, size), f32),
+            pltpu.VMEM((groups, rows, span), f32),
+            half,
+            half,
+            half,
+            half,
+            pltpu.VMEM((blocks, BLOCK), f32),
+            pltpu.VMEM((count, blocks, BLOCK), f32),
+            dma((count,)),
+            dma((count,)),
+            dma((groups, count)),
+            dma((groups, count)),
+            dma((2, groups, count)),
+            dma((2, groups, count)),
+            dma((3, groups)),
         ],
-        scratch_shapes=[pltpu.VMEM((group, size, size), f32)],
-        compiler_params=params,
-        cost_estimate=cost(160),
+        compiler_params=pltpu.CompilerParams(
+            dimension_semantics=("arbitrary", "arbitrary"),
+            collective_id=2,
+            has_side_effects=True,
+            vmem_limit_bytes=VMEM,
+        ),
         name="block_grads",
     )(
         query_raw, key_raw, out_grad, crow, ccol, inv, gain_row,
         inverse, weight, initial, trans, adjoint, inner, prefix, incoming, outgoing,
-    )
-
-    owned = jax.ShapeDtypeStruct((rows // count, full), jnp.bfloat16)
-    return pl.pallas_call(
-        functools.partial(finish_kernel, count, full),
-        in_specs=[anywhere] * 4 + [in_vmem] * 2,
-        out_specs=[anywhere] * 3,
-        out_shape=[owned] * 3,
-        scratch_shapes=[
-            pltpu.VMEM((rows, width), f32),
-            pltpu.VMEM((rows, width), jnp.bfloat16),
-            pltpu.VMEM((rows, width), jnp.bfloat16),
-            pltpu.VMEM((count, blocks, BLOCK), f32),
-            dma((2,)),
-            dma((count,)),
-            dma((count,)),
-            dma((3, count)),
-            dma((3, count)),
-            dma((3,)),
-        ],
-        compiler_params=pltpu.CompilerParams(
-            collective_id=2, has_side_effects=True, vmem_limit_bytes=VMEM
-        ),
-        name="send_gradients",
-    )(
-        scaled, query_raw, key_grad, value_grad, inv_rows.T,
-        jnp.sum(correction, axis=0).reshape(blocks, BLOCK),
+        inv_rows.T,
     )
 
 

time: 221 us -> 200 us (0.905)
  Pallas kernels: 200 us -> 183 us
  local copies, waits for them, and re-layouts: 15.1 us -> 10.3 us
    pallas_call x2 -> x1, Pallas kernels: 116 us -> 99.5 us  [per_device(): pl.pallas_call(functools.partial(grads_kernel, count, full), grid=grid, i...]
    unnamed x21 -> x17, local copies, waits for them, and re-layouts: 12.4 us -> 9.2 us
where the time goes in v4:
time: 200 us
  Pallas kernels  183 us (92%)
  local copies, waits for them, and re-layouts  10.3 us (5%)
  other arithmetic  5.63 us (3%)
    pallas_call x1, Pallas kernels, per_device(): pl.pallas_call(functools.partial(grads_kernel, count, full), grid=grid, i...  99.5 us
    pallas_call x1, Pallas kernels, per_device(): pl.pallas_call(maps_kernel, grid=grid, in_specs=[s['raw'], s['raw'], s['c...  28.8 us
    pallas_call x1, Pallas kernels, per_device(): pl.pallas_call(functools.partial(states_kernel, turns), in_specs=[in_vmem...  27 us
    pallas_call x1, Pallas kernels, per_device(): pl.pallas_call(chain_kernel, grid=grid, in_specs=[s['raw']] * 3 + [s['cro...  20.5 us
    unnamed x17, local copies, waits for them, and re-layouts  9.2 us
    pallas_call x1, Pallas kernels, per_device(): pl.pallas_call(functools.partial(total_kernel, count), in_specs=[in_vmem]...  7.23 us

profile of v4, /device:TPU:1, one launch (start us, length us, event | category | flops | bytes accessed | tf_op | source)
XLA Modules:
  0.0 199.7 jit_solution(14483559090219939811)
XLA Ops:
  0.7 2.7 %multiply_reduce_fusion = f32[1024]{0:T(1024)} fusion(bf16[1024,1024]{1,0:T(8,128)(2,1)} %q_ref.3), kind=kLoop, calls=%fused_computation | loop fusion | flops 3144704 | bytes 2101248 | tf_op jit(solution)/shard_map/reduce_sum | solution.py:495
  3.3 7.2 %token_squares.1 = f32[8,128]{1,0:T(8,128)} custom-call(f32[8,128]{1,0:T(8,128)} %bitcast.23), custom_call_target="tpu_custom_call" | custom-call | tf_op jit(solution)/shard_map/token_squares/pallas_call | solution.py:487
  10.6 0.7 add_rsqrt_fusion
  11.2 0.0 copy-done.5
  11.3 2.3 %reduce_window_sum.11 = f32[8,8,128]{2,1,0:T(8,128)S(1)} reduce-window(f32[8,8,128]{2,1,0:T(8,128)S(1)} %copy.24, f32[]{:T(128)} %constant.4.clone.1), window={size=1x1x128 pad=0_0x0_0x127_0}, to_apply=%region_0.0 | reduce-window | flops 1040384 | bytes 65540 | tf_op jit(solution)/shard_map/jit(cumsum)/reduce_window_sum | solution.py:501
  13.6 0.1 copy.29
  13.7 0.2 copy.28.gcol_ref
  13.9 0.2 copy.30.inv_ref
  14.1 0.2 copy.26
  14.3 0.4 copy.25
  14.7 0.0 copy-start.1
  14.7 1.6 copy-done.1
  16.3 1.6 copy-done.2
  17.9 28.8 %block_maps.1 = (f32[8,8,128,128]{3,2,1,0:T(8,128)}, f32[8,8,128,128]{3,2,1,0:T(8,128)}, f32[8,8,128,128]{3,2,1,0:T(8,128)}, f32[8,8,128,128]{3,2,1,0:T(8,128)}, f32[8,8,128,128]{3,2,1,0:T(8,128)}) custom-call(bf16[1024,1024]{1,0:T(8,128)(2,1)S(1)} %copy-done.1, bf16[1024,1024]{1,0:T(8,128)(2,1)S(1)} %copy-done.2, f32[8,1,1024]{2,1,0:T(1,128)S(1)} %bitcast.13, ...), custom_call_target="tpu_custom_call" | custom-call | flops 42949672960 | bytes 25165824 | tf_op jit(solution)/shard_map/block_maps/pallas_call | solution.py:536
  46.7 0.0 copy-done
  46.7 20.5 %device_maps.1 = (f32[8,8,128,128]{3,2,1,0:T(8,128)}, f32[8,8,128,128]{3,2,1,0:T(8,128)}, f32[8,8,128,256]{3,2,1,0:T(8,128)}, f32[8,128,256]{2,1,0:T(8,128)S(1)}, f32[8,128,128]{2,1,0:T(8,128)S(1)}) custom-call(bf16[1024,1024]{1,0:T(8,128)(2,1)S(1)} %copy-done, bf16[1024,1024]{1,0:T(8,128)(2,1)} %k_ref.5, bf16[1024,1024]{1,0:T(8,128)(2,1)} %g_ref.3, ...), custom_call_target="tpu_custom_call" | custom-call | flops 21474836480 | bytes 25165824 | tf_op jit(solution)/shard_map/device_maps/pallas_call | solution.py:546
  67.2 27.0 %device_states.1 = (f32[8,128,128]{2,1,0:T(8,128)S(1)}, f32[8,128,128]{2,1,0:T(8,128)S(1)}) custom-call(f32[8,128,256]{2,1,0:T(8,128)S(1)} %get-tuple-element.23.map_ref, f32[8,128,128]{2,1,0:T(8,128)S(1)} %get-tuple-element.24.adj_ref), custom_call_target="tpu_custom_call" | custom-call | tf_op jit(solution)/shard_map/device_states/pallas_call | solution.py:568
  94.2 99.5 %block_grads.1 = (bf16[128,8192]{1,0:T(8,128)(2,1)S(1)}, bf16[128,8192]{1,0:T(8,128)(2,1)}, bf16[128,8192]{1,0:T(8,128)(2,1)}) custom-call(bf16[1024,1024]{1,0:T(8,128)(2,1)} %q_ref.3, bf16[1024,1024]{1,0:T(8,128)(2,1)} %k_ref.5, bf16[1024,1024]{1,0:T(8,128)(2,1)} %g_ref.3, f32[8,1,1024]{2,1,0:T(1,128)S(1)} %bitcast.15, f32[2,1024,4]{2,1,0:T(8,128)S(1)} %bitcast.12, ...), custom_call_target="tpu_custom_call" | custom-call | tf_op jit(solution)/shard_map/block_grads/pallas_call | solution.py:588
  193.7 0.0 copy-start.4
  193.7 1.3 copy.34
  195.1 1.0 copy-done.4
  196.1 1.3 copy.35
  197.4 1.0 copy-done.3
  198.4 1.3 copy.36
  (9 shorter events, 0.0 us)
Async XLA Ops:
  0.6 10.6 %copy-start.5 = (f32[8,1024]{1,0:T(8,128)S(1)}, f32[8,1024]{1,0:T(8,128)}, u32[]{:S(2)}) copy-start(f32[8,1024]{1,0:T(8,128)} %param.10) | copy-start | bytes 98308
  0.6 10.6 %copy-start.6 = (f32[1024]{0:T(1024)S(1)}, f32[1024]{0:T(1024)}, u32[]{:S(2)}) copy-start(f32[1024]{0:T(1024)} %param.9) | copy-start | bytes 12292
  14.7 1.6 copy-start.1
  16.3 1.6 copy-start.2
  17.9 28.8 %copy-start = (bf16[1024,1024]{1,0:T(8,128)(2,1)S(1)}, bf16[1024,1024]{1,0:T(8,128)(2,1)}, u32[]{:S(2)}) copy-start(bf16[1024,1024]{1,0:T(8,128)(2,1)} %q_ref.3) | copy-start | bytes 6291460
  193.7 2.3 %copy-start.4 = (bf16[128,8192]{1,0:T(8,128)(2,1)S(1)}, bf16[128,8192]{1,0:T(8,128)(2,1)}, u32[]{:S(2)}) copy-start(bf16[128,8192]{1,0:T(8,128)(2,1)} %get-tuple-element.33) | copy-start | bytes 6291460
  196.1 2.3 %copy-start.3 = (bf16[128,8192]{1,0:T(8,128)(2,1)S(1)}, bf16[128,8192]{1,0:T(8,128)(2,1)}, u32[]{:S(2)}) copy-start(bf16[128,8192]{1,0:T(8,128)(2,1)} %get-tuple-element.34) | copy-start | bytes 6291460
